TPU v7x, 512 devices: a whole 4x8x8 slice. The times are simulated.
512 devices in a mesh: leaf: 512 (over x, z, y, core).
Axes of the slice: x: 4, y: 8, z: 8, core: 2. Of those that a mesh axis runs over, the one named last changes fastest.
Arguments:
- values: bfloat16 [1572864, 128], P('leaf'), may hold values from -6 to 6
- points: float32 [8, 1572864], P(None, 'leaf'), may hold values from -6 to 6
- tree_order: int32 [512, 3072], P('leaf'), may hold values from 0 to 3071, each once within a row
- leaf_sizes: int32 [512, 16], P('leaf'), may hold values from 1 to 256, 3072 in all within a row
- leaf_basis: bfloat16 [8192, 256, 128], P('leaf'), may hold values from -0.375 to 0.375
- local_transfer: bfloat16 [7680, 2, 128, 128], P('leaf'), may hold values from -0.4375 to 0.4375
- local_coupling: bfloat16 [7680, 128, 128], P('leaf'), may hold values from -0.5 to 0.5
- cross_transfer: bfloat16 [512, 2, 128, 128], P('leaf'), may hold values from -0.4375 to 0.4375
- cross_coupling: bfloat16 [512, 128, 128], P('leaf'), may hold values from -0.5 to 0.5
Outputs:
- product_values: bfloat16 [1572864, 128], P('leaf')
Inputs may be any that keep to these rules, and one draw needn't show every extreme that they name: `tree_order`: each row is a permutation of 0 .. 3071. `leaf_sizes`: each row sums to 3072; its largest entry is 256.
All inputs are finite; a program needn't handle non-finite values.
Results may differ from a plain program's by a relative error of at most 0.0048.
Values sent between devices are 32-bit elements; how exact they have to be, the bound alone decides.
A program may use at most 64 MiB of HBM per device.

v0:
```python
import jax
import jax.numpy as jnp
from jax import lax
from jax.sharding import PartitionSpec as P

kernel_scale = 8.0
ridge_shift = 1.0
exact_products = lax.Precision.HIGHEST


def shifted(block, axis, distance):
    devices = range(lax.axis_size(axis))
    route = [(i - distance, i) for i in devices if i - distance in devices]
    return lax.ppermute(block, axis, route)


def arrange(values, points, tree_order, leaf_sizes, leaf_width):
    point_count = values.shape[0]
    starts = jnp.cumsum(leaf_sizes) - leaf_sizes
    within = jnp.arange(leaf_width, dtype=jnp.int32)
    position = starts[:, None] + within[None, :]
    inside = within[None, :] < leaf_sizes[:, None]
    source = tree_order[jnp.clip(position, 0, point_count - 1)]
    leaf_rows = jnp.where(inside[:, :, None], values[source], jnp.zeros((), values.dtype))
    leaf_points = points[:, source]
    target = jnp.where(inside, source, point_count)
    return (leaf_rows, leaf_points, target)


def leaf_nearby(leaf_rows, leaf_points):
    squares = jnp.sum(leaf_points * leaf_points, axis=0)
    inner = jnp.einsum("dta,dtb->tab", leaf_points, leaf_points, precision=exact_products)
    distance = squares[:, :, None] + squares[:, None, :] - 2.0 * inner
    unit = jnp.eye(leaf_points.shape[2], dtype=jnp.float32)
    kernel = (jnp.exp(-distance / kernel_scale) + ridge_shift * unit).astype(jnp.bfloat16)
    return jnp.einsum("tab,tbr->tar", kernel, leaf_rows, preferred_element_type=jnp.float32)


def climb(coefficients, transfer, coupling):
    transfer = transfer.astype(jnp.float32)
    coupling = coupling.astype(jnp.float32)
    left_part = coefficients[0::2]
    right_part = coefficients[1::2]
    parent = jnp.einsum("jkq,jkr->jqr", transfer[:, 0], left_part, precision=exact_products)
    parent = parent + jnp.einsum(
        "jkq,jkr->jqr", transfer[:, 1], right_part, precision=exact_products
    )
    toward_left = jnp.einsum("jqk,jkr->jqr", coupling, right_part, precision=exact_products)
    toward_right = jnp.einsum("jkq,jkr->jqr", coupling, left_part, precision=exact_products)
    return (parent, toward_left, toward_right)


def descend(field, toward_left, toward_right, transfer):
    transfer = transfer.astype(jnp.float32)
    left_field = toward_left + jnp.einsum(
        "jqk,jkr->jqr", transfer[:, 0], field, precision=exact_products
    )
    right_field = toward_right + jnp.einsum(
        "jqk,jkr->jqr", transfer[:, 1], field, precision=exact_products
    )
    return jnp.stack([left_field, right_field], 1).reshape((-1,) + field.shape[1:])


def body(
    values,
    points,
    tree_order,
    leaf_sizes,
    leaf_basis,
    local_transfer,
    local_coupling,
    cross_transfer,
    cross_coupling,
):
    devices = lax.axis_size("leaf")
    levels = devices.bit_length() - 1
    device_index = lax.axis_index("leaf")
    leaf_count = leaf_basis.shape[0]
    leaf_width = leaf_basis.shape[1]
    rhs_width = values.shape[1]
    top_levels = 0
    split_height = levels - top_levels
    leaf_rows, leaf_points, target = arrange(
        values, points, tree_order[0], leaf_sizes[0], leaf_width
    )
    nearby = None
    coefficients = jnp.einsum(
        "tak,tar->tkr", leaf_basis, leaf_rows, preferred_element_type=jnp.float32
    )
    stored = []
    offset = 0
    nodes = leaf_count
    for section in range(leaf_count.bit_length() - 1):
        half = nodes // 2
        coefficients, toward_left, toward_right = climb(
            coefficients,
            local_transfer[offset : offset + half],
            local_coupling[offset : offset + half],
        )
        stored.append((toward_left, toward_right, offset, half))
        offset = offset + half
        nodes = half
    current = coefficients
    kept_left = []
    kept_right = []
    for height in range(1, split_height + 1):
        reach = 2 ** (height - 1)
        arrived = shifted(current, "leaf", reach)
        joined = jnp.concatenate([arrived, current], 0)
        parent, toward_left, toward_right = climb(joined, cross_transfer, cross_coupling)
        packed = jnp.concatenate([parent, toward_left], 0)
        returned = shifted(packed, "leaf", -reach)
        holder = device_index % 2**height == 0
        current = jnp.where(holder, returned[0:1], current)
        kept_left.append(returned[1:2])
        kept_right.append(toward_right)
    inner_field = jnp.zeros_like(current)
    empty_term = jnp.zeros_like(current)
    for height in range(split_height, 0, -1):
        reach = 2 ** (height - 1)
        pushed = shifted(inner_field, "leaf", reach)
        both_fields = descend(pushed, empty_term, kept_right[height - 1], cross_transfer)
        carried = shifted(both_fields[0:1], "leaf", -reach)
        left_field = kept_left[height - 1] + carried
        position = device_index % 2**height
        inner_field = jnp.where(
            position == 0, left_field, jnp.where(position == reach, both_fields[1:2], inner_field)
        )
    local_field = inner_field
    for toward_left, toward_right, offset, half in reversed(stored):
        local_field = descend(
            local_field, toward_left, toward_right, local_transfer[offset : offset + half]
        )
    nearby = leaf_nearby(leaf_rows, leaf_points)
    distant = jnp.einsum(
        "tak,tkr->tar",
        leaf_basis,
        local_field.astype(jnp.bfloat16),
        preferred_element_type=jnp.float32,
    )
    total = nearby + distant
    result = (
        jnp.zeros((values.shape[0], rhs_width), jnp.float32)
        .at[target.reshape(-1)]
        .set(total.reshape(-1, rhs_width), mode="drop")
    )
    return result.astype(jnp.bfloat16)


def solution(mesh):
    in_specs = (
        P("leaf", None),
        P(None, "leaf"),
        P("leaf", None),
        P("leaf", None),
        P("leaf", None, None),
        P("leaf", None, None, None),
        P("leaf", None, None),
        P("leaf", None, None, None),
        P("leaf", None, None),
    )
    out_specs = P("leaf", None)
    return jax.shard_map(body, mesh=mesh, in_specs=in_specs, out_specs=out_specs, check_vma=False)
```

profile of v0, /device:TPU:2, one launch (start us, length us, event | category | flops | bytes accessed | tf_op | source)
XLA Modules:
  0.0 434.0 jit_solution(15445289272296706685)
XLA Ops:
  2.5 23.0 %gather_fusion = s32[4096]{0:T(1024)S(1)} fusion(s32[3072]{0:T(1024)S(1)} %bitcast.595, s32[4096]{0:T(1024)S(1)} %broadcast_clamp_fusion.1), kind=kCustom, calls=%fused_computation | custom fusion | bytes 49152 | tf_op jit(solution)/shard_map/gather | solution.py:23
  25.6 15.0 %gather_fusion.2 = bf16[4096,128]{1,0:T(8,128)(2,1)} fusion(bf16[3072,128]{1,0:T(8,128)(2,1)S(1)} %copy-done.2, s32[4096]{0:T(1024)S(1)} %broadcast_clamp_fusion), kind=kCustom, calls=%fused_computation.2 | custom fusion | bytes 2113536 | tf_op jit(solution)/shard_map/gather | solution.py:24
  48.6 12.9 %collective-permute-done = f32[1,128,128]{1,2,0:T(8,128)S(1)} collective-permute-done((f32[1,128,128]{1,2,0:T(8,128)S(1)}, f32[1,128,128]{1,2,0:T(8,128)S(1)}, u32[]{:S(2)}, u32[]{:S(2)}) %collective-permute-start) | collective-permute-done | bytes 65568 | tf_op jit(solution)/shard_map/ppermute | solution.py:14
  70.7 8.5 %collective-permute-done.2 = f32[1,128,128]{1,2,0:T(8,128)S(1)} collective-permute-done((f32[1,128,128]{1,2,0:T(8,128)S(1)}, f32[1,128,128]{1,2,0:T(8,128)S(1)}, u32[]{:S(2)}, u32[]{:S(2)}) %collective-permute-start.2) | collective-permute-done | bytes 65568 | tf_op jit(solution)/shard_map/ppermute | solution.py:14
  91.1 10.1 %collective-permute-done.4 = f32[1,128,128]{1,2,0:T(8,128)S(1)} collective-permute-done((f32[1,128,128]{1,2,0:T(8,128)S(1)}, f32[1,128,128]{1,2,0:T(8,128)S(1)}, u32[]{:S(2)}, u32[]{:S(2)}) %collective-permute-start.4) | collective-permute-done | bytes 65568 | tf_op jit(solution)/shard_map/ppermute | solution.py:14
  115.4 11.0 %collective-permute-done.6 = f32[1,128,128]{1,2,0:T(8,128)S(1)} collective-permute-done((f32[1,128,128]{1,2,0:T(8,128)S(1)}, f32[1,128,128]{1,2,0:T(8,128)S(1)}, u32[]{:S(2)}, u32[]{:S(2)}) %collective-permute-start.6) | collective-permute-done | bytes 65568 | tf_op jit(solution)/shard_map/ppermute | solution.py:14
  129.3 8.2 %collective-permute-done.7 = f32[2,128,128]{1,2,0:T(8,128)S(1)} collective-permute-done((f32[2,128,128]{1,2,0:T(8,128)S(1)}, f32[2,128,128]{1,2,0:T(8,128)S(1)}, u32[]{:S(2)}, u32[]{:S(2)}) %collective-permute-start.7) | collective-permute-done | bytes 131104 | tf_op jit(solution)/shard_map/ppermute | solution.py:14
  140.5 6.1 %collective-permute-done.8 = f32[1,128,128]{1,2,0:T(8,128)S(1)} collective-permute-done((f32[1,128,128]{1,2,0:T(8,128)S(1)}, f32[1,128,128]{1,2,0:T(8,128)S(1)}, u32[]{:S(2)}, u32[]{:S(2)}) %collective-permute-start.8) | collective-permute-done | bytes 65568 | tf_op jit(solution)/shard_map/ppermute | solution.py:14
  151.9 15.6 %gather_fusion.1 = f32[4096,8]{1,0:T(8,128)} fusion(f32[8,3072]{0,1:T(8,128)} %copy.22, s32[4096]{0:T(1024)S(1)} %broadcast_clamp_fusion), kind=kCustom, calls=%fused_computation.1 | custom fusion | bytes 278528 | tf_op jit(solution)/shard_map/gather | solution.py:25
  170.7 7.0 %collective-permute-done.10 = f32[1,128,128]{1,2,0:T(8,128)S(1)} collective-permute-done((f32[1,128,128]{1,2,0:T(8,128)S(1)}, f32[1,128,128]{1,2,0:T(8,128)S(1)}, u32[]{:S(2)}, u32[]{:S(2)}) %collective-permute-start.10) | collective-permute-done | bytes 65568 | tf_op jit(solution)/shard_map/ppermute | solution.py:14
  193.6 5.7 %collective-permute-done.12 = f32[1,128,128]{1,2,0:T(8,128)S(1)} collective-permute-done((f32[1,128,128]{1,2,0:T(8,128)S(1)}, f32[1,128,128]{1,2,0:T(8,128)S(1)}, u32[]{:S(2)}, u32[]{:S(2)}) %collective-permute-start.12) | collective-permute-done | bytes 65568 | tf_op jit(solution)/shard_map/ppermute | solution.py:14
  200.5 5.5 %collective-permute-start.13 = (f32[2,128,128]{1,2,0:T(8,128)}, f32[2,128,128]{1,2,0:T(8,128)}, u32[]{:S(2)}, u32[]{:S(2)}) collective-permute-start(f32[2,128,128]{1,2,0:T(8,128)} %pad_maximum_fusion.9), channel_id=1, source_target_pairs={{64,0},{65,1},{66,2},{67,3},{68,4},{69,5},{70,6},{71,7},{72,8},{73... | collective-permute-start | bytes 393224 | tf_op jit(solution)/shard_map/ppermute | solution.py:14
  206.1 8.3 %add_convert_fusion = bf16[16,256,256]{2,1,0:T(8,128)(2,1)} fusion(f32[8,16,256]{0,2,1:T(8,128)} %bitcast.598, f32[256,256]{1,0:T(8,128)S(1)} %fusion.56, f32[16,256]{1,0:T(8,128)S(1)} %multiply_reduce_fusion), kind=kOutput, calls=%fused_computation.4 | convolution fusion | flops 108003328 | bytes 2506752 | tf_op jit(solution)/shard_map/dta,dtb->tab/dot_general | solution.py:32
  215.4 6.7 %collective-permute-start.14 = (f32[1,128,128]{1,2,0:T(8,128)S(1)}, f32[1,128,128]{1,2,0:T(8,128)S(1)}, u32[]{:S(2)}, u32[]{:S(2)}) collective-permute-start(f32[1,128,128]{1,2,0:T(8,128)S(1)} %slice_select_fusion.1), channel_id=1, source_target_pairs={{0,128},{1,129},{2,130},{3,131},{4,132},{5,133},{6,134},{7,135},{8... | collective-permute-start | bytes 196616 | tf_op jit(solution)/shard_map/ppermute | solution.py:14
  234.9 6.4 %collective-permute-start.16 = (f32[1,128,128]{1,2,0:T(8,128)S(1)}, f32[1,128,128]{1,2,0:T(8,128)S(1)}, u32[]{:S(2)}, u32[]{:S(2)}) collective-permute-start(f32[1,128,128]{1,2,0:T(8,128)S(1)} %slice_select_fusion), channel_id=1, source_target_pairs={{0,256},{1,257},{2,258},{3,259},{4,260},{5,261},{6,262},{7,263},{8... | collective-permute-start | bytes 196616 | tf_op jit(solution)/shard_map/ppermute | solution.py:14
  245.9 6.0 %collective-permute-done.17 = f32[2,128,128]{1,2,0:T(8,128)S(1)} collective-permute-done((f32[2,128,128]{1,2,0:T(8,128)S(1)}, f32[2,128,128]{1,2,0:T(8,128)S(1)}, u32[]{:S(2)}, u32[]{:S(2)}) %collective-permute-start.17) | collective-permute-done | bytes 131104 | tf_op jit(solution)/shard_map/ppermute | solution.py:14
  268.1 6.8 %collective-permute-start.22 = (f32[1,128,128]{1,2,0:T(8,128)}, f32[1,128,128]{1,2,0:T(8,128)}, u32[]{:S(2)}, u32[]{:S(2)}) collective-permute-start(f32[1,128,128]{1,2,0:T(8,128)} %fusion.88), channel_id=1, source_target_pairs={{0,64},{1,65},{2,66},{3,67},{4,68},{5,69},{6,70},{7,71},{8,72},{9,... | collective-permute-start | bytes 196616 | tf_op jit(solution)/shard_map/ppermute | solution.py:14
  304.3 5.5 %collective-permute-done.25 = f32[1,128,128]{1,2,0:T(8,128)S(1)} collective-permute-done((f32[1,128,128]{1,2,0:T(8,128)S(1)}, f32[1,128,128]{1,2,0:T(8,128)S(1)}, u32[]{:S(2)}, u32[]{:S(2)}) %collective-permute-start.25) | collective-permute-done | bytes 65568 | tf_op jit(solution)/shard_map/ppermute | solution.py:14
  330.4 10.4 %collective-permute-done.28 = f32[1,128,128]{1,2,0:T(8,128)S(1)} collective-permute-done((f32[1,128,128]{1,2,0:T(8,128)S(1)}, f32[1,128,128]{1,2,0:T(8,128)S(1)}, u32[]{:S(2)}, u32[]{:S(2)}) %collective-permute-start.28) | collective-permute-done | bytes 65568 | tf_op jit(solution)/shard_map/ppermute | solution.py:14
  343.1 8.4 %collective-permute-done.29 = f32[1,128,128]{1,2,0:T(8,128)S(1)} collective-permute-done((f32[1,128,128]{1,2,0:T(8,128)S(1)}, f32[1,128,128]{1,2,0:T(8,128)S(1)}, u32[]{:S(2)}, u32[]{:S(2)}) %collective-permute-start.29) | collective-permute-done | bytes 65568 | tf_op jit(solution)/shard_map/ppermute | solution.py:14
  356.2 7.6 %collective-permute-done.30 = f32[1,128,128]{1,2,0:T(8,128)S(1)} collective-permute-done((f32[1,128,128]{1,2,0:T(8,128)S(1)}, f32[1,128,128]{1,2,0:T(8,128)S(1)}, u32[]{:S(2)}, u32[]{:S(2)}) %collective-permute-start.30) | collective-permute-done | bytes 65568 | tf_op jit(solution)/shard_map/ppermute | solution.py:14
  375.2 7.4 %collective-permute-done.32 = f32[1,128,128]{1,2,0:T(8,128)S(1)} collective-permute-done((f32[1,128,128]{1,2,0:T(8,128)S(1)}, f32[1,128,128]{1,2,0:T(8,128)S(1)}, u32[]{:S(2)}, u32[]{:S(2)}) %collective-permute-start.32) | collective-permute-done | bytes 65568 | tf_op jit(solution)/shard_map/ppermute | solution.py:14
  394.4 6.4 %collective-permute-done.34 = f32[1,128,128]{1,2,0:T(8,128)S(1)} collective-permute-done((f32[1,128,128]{1,2,0:T(8,128)}, f32[1,128,128]{1,2,0:T(8,128)S(1)}, u32[]{:S(2)}, u32[]{:S(2)}) %collective-permute-start.34) | collective-permute-done | bytes 65568 | tf_op jit(solution)/shard_map/ppermute | solution.py:14
  421.7 11.3 %scatter_custom_fusion = f32[3072,128]{1,0:T(8,128)S(1)} fusion(s32[4096]{0:T(1024)S(1)} %bitcast.607, f32[4096,128]{1,0:T(8,128)} %bitcast.601, f32[]{:T(128)} %constant.111.clone.1), kind=kCustom, calls=%fused_computation.98 | custom fusion | bytes 1573376 | tf_op jit(solution)/shard_map/scatter | solution.py:145
  (245 shorter events, 212.8 us)
Async XLA Ops:
  46.3 15.2 %collective-permute-start = (f32[1,128,128]{1,2,0:T(8,128)S(1)}, f32[1,128,128]{1,2,0:T(8,128)S(1)}, u32[]{:S(2)}, u32[]{:S(2)}) collective-permute-start(f32[1,128,128]{1,2,0:T(8,128)S(1)} %bitcast.603), channel_id=1, source_target_pairs={{0,1},{1,2},{2,3},{3,4},{4,5},{5,6},{6,7},{7,8},{8,9},{9,10},{10,1... | collective-permute-start | bytes 196616 | tf_op jit(solution)/shard_map/ppermute | solution.py:14
  68.6 10.6 %collective-permute-start.2 = (f32[1,128,128]{1,2,0:T(8,128)S(1)}, f32[1,128,128]{1,2,0:T(8,128)S(1)}, u32[]{:S(2)}, u32[]{:S(2)}) collective-permute-start(f32[1,128,128]{1,2,0:T(8,128)S(1)} %slice_select_fusion.7), channel_id=1, source_target_pairs={{0,2},{1,3},{2,4},{3,5},{4,6},{5,7},{6,8},{7,9},{8,10},{9,11},{10,... | collective-permute-start | bytes 196616 | tf_op jit(solution)/shard_map/ppermute | solution.py:14
  88.9 12.3 %collective-permute-start.4 = (f32[1,128,128]{1,2,0:T(8,128)S(1)}, f32[1,128,128]{1,2,0:T(8,128)S(1)}, u32[]{:S(2)}, u32[]{:S(2)}) collective-permute-start(f32[1,128,128]{1,2,0:T(8,128)S(1)} %slice_select_fusion.6), channel_id=1, source_target_pairs={{0,4},{1,5},{2,6},{3,7},{4,8},{5,9},{6,10},{7,11},{8,12},{9,13},{1... | collective-permute-start | bytes 196616 | tf_op jit(solution)/shard_map/ppermute | solution.py:14
  102.5 9.7 %collective-permute-start.5 = (f32[2,128,128]{1,2,0:T(8,128)}, f32[2,128,128]{1,2,0:T(8,128)}, u32[]{:S(2)}, u32[]{:S(2)}) collective-permute-start(f32[2,128,128]{1,2,0:T(8,128)} %pad_maximum_fusion.5), channel_id=1, source_target_pairs={{4,0},{5,1},{6,2},{7,3},{8,4},{9,5},{10,6},{11,7},{12,8},{13,9},{1... | collective-permute-start | bytes 393224 | tf_op jit(solution)/shard_map/ppermute | solution.py:14
  105.0 126.4 %collective-permute-start.18 = (f32[1,128,128]{2,1,0:T(8,128)}, f32[1,128,128]{2,1,0:T(8,128)}, u32[]{:S(2)}, u32[]{:S(2)}) collective-permute-start(f32[1,128,128]{2,1,0:T(8,128)} %broadcast_in_dim.36), channel_id=1, source_target_pairs={{0,256},{1,257},{2,258},{3,259},{4,260},{5,261},{6,262},{7,263},{8... | collective-permute-start | bytes 196616 | tf_op jit(solution)/shard_map/ppermute | solution.py:14
  113.2 13.2 %collective-permute-start.6 = (f32[1,128,128]{1,2,0:T(8,128)S(1)}, f32[1,128,128]{1,2,0:T(8,128)S(1)}, u32[]{:S(2)}, u32[]{:S(2)}) collective-permute-start(f32[1,128,128]{1,2,0:T(8,128)S(1)} %slice_select_fusion.5), channel_id=1, source_target_pairs={{0,8},{1,9},{2,10},{3,11},{4,12},{5,13},{6,14},{7,15},{8,16},{9,17... | collective-permute-start | bytes 196616 | tf_op jit(solution)/shard_map/ppermute | solution.py:14
  126.6 10.9 %collective-permute-start.7 = (f32[2,128,128]{1,2,0:T(8,128)S(1)}, f32[2,128,128]{1,2,0:T(8,128)S(1)}, u32[]{:S(2)}, u32[]{:S(2)}) collective-permute-start(f32[2,128,128]{1,2,0:T(8,128)S(1)} %pad_maximum_fusion.6), channel_id=1, source_target_pairs={{8,0},{9,1},{10,2},{11,3},{12,4},{13,5},{14,6},{15,7},{16,8},{17,9... | collective-permute-start | bytes 393224 | tf_op jit(solution)/shard_map/ppermute | solution.py:14
  147.5 20.1 %collective-permute-start.9 = (f32[2,128,128]{1,2,0:T(8,128)}, f32[2,128,128]{1,2,0:T(8,128)}, u32[]{:S(2)}, u32[]{:S(2)}) collective-permute-start(f32[2,128,128]{1,2,0:T(8,128)} %pad_maximum_fusion.7), channel_id=1, source_target_pairs={{16,0},{17,1},{18,2},{19,3},{20,4},{21,5},{22,6},{23,7},{24,8},{25... | collective-permute-start | bytes 393224 | tf_op jit(solution)/shard_map/ppermute | solution.py:14
  168.6 9.2 %collective-permute-start.10 = (f32[1,128,128]{1,2,0:T(8,128)S(1)}, f32[1,128,128]{1,2,0:T(8,128)S(1)}, u32[]{:S(2)}, u32[]{:S(2)}) collective-permute-start(f32[1,128,128]{1,2,0:T(8,128)S(1)} %slice_select_fusion.3), channel_id=1, source_target_pairs={{0,32},{1,33},{2,34},{3,35},{4,36},{5,37},{6,38},{7,39},{8,40},{9,... | collective-permute-start | bytes 196616 | tf_op jit(solution)/shard_map/ppermute | solution.py:14
  188.3 11.0 %collective-permute-start.12 = (f32[1,128,128]{1,2,0:T(8,128)S(1)}, f32[1,128,128]{1,2,0:T(8,128)S(1)}, u32[]{:S(2)}, u32[]{:S(2)}) collective-permute-start(f32[1,128,128]{1,2,0:T(8,128)S(1)} %slice_select_fusion.2), channel_id=1, source_target_pairs={{0,64},{1,65},{2,66},{3,67},{4,68},{5,69},{6,70},{7,71},{8,72},{9,... | collective-permute-start | bytes 196616 | tf_op jit(solution)/shard_map/ppermute | solution.py:14
  200.5 13.8 %collective-permute-start.13 = (f32[2,128,128]{1,2,0:T(8,128)}, f32[2,128,128]{1,2,0:T(8,128)}, u32[]{:S(2)}, u32[]{:S(2)}) collective-permute-start(f32[2,128,128]{1,2,0:T(8,128)} %pad_maximum_fusion.9), channel_id=1, source_target_pairs={{64,0},{65,1},{66,2},{67,3},{68,4},{69,5},{70,6},{71,7},{72,8},{73... | collective-permute-start | bytes 393224 | tf_op jit(solution)/shard_map/ppermute | solution.py:14
  215.4 9.2 %collective-permute-start.14 = (f32[1,128,128]{1,2,0:T(8,128)S(1)}, f32[1,128,128]{1,2,0:T(8,128)S(1)}, u32[]{:S(2)}, u32[]{:S(2)}) collective-permute-start(f32[1,128,128]{1,2,0:T(8,128)S(1)} %slice_select_fusion.1), channel_id=1, source_target_pairs={{0,128},{1,129},{2,130},{3,131},{4,132},{5,133},{6,134},{7,135},{8... | collective-permute-start | bytes 196616 | tf_op jit(solution)/shard_map/ppermute | solution.py:14
  232.5 13.3 %collective-permute-start.19 = (f32[1,128,128]{1,2,0:T(8,128)S(1)}, f32[1,128,128]{1,2,0:T(8,128)S(1)}, u32[]{:S(2)}, u32[]{:S(2)}) collective-permute-start(f32[1,128,128]{1,2,0:T(8,128)S(1)} %convolution_bitcast_fusion.9), channel_id=1, source_target_pairs={{256,0},{257,1},{258,2},{259,3},{260,4},{261,5},{262,6},{263,7},{2... | collective-permute-start | bytes 196616 | tf_op jit(solution)/shard_map/ppermute | solution.py:14
  234.9 8.3 %collective-permute-start.16 = (f32[1,128,128]{1,2,0:T(8,128)S(1)}, f32[1,128,128]{1,2,0:T(8,128)S(1)}, u32[]{:S(2)}, u32[]{:S(2)}) collective-permute-start(f32[1,128,128]{1,2,0:T(8,128)S(1)} %slice_select_fusion), channel_id=1, source_target_pairs={{0,256},{1,257},{2,258},{3,259},{4,260},{5,261},{6,262},{7,263},{8... | collective-permute-start | bytes 196616 | tf_op jit(solution)/shard_map/ppermute | solution.py:14
  243.5 8.4 %collective-permute-start.17 = (f32[2,128,128]{1,2,0:T(8,128)S(1)}, f32[2,128,128]{1,2,0:T(8,128)S(1)}, u32[]{:S(2)}, u32[]{:S(2)}) collective-permute-start(f32[2,128,128]{1,2,0:T(8,128)S(1)} %pad_maximum_fusion.11), channel_id=1, source_target_pairs={{256,0},{257,1},{258,2},{259,3},{260,4},{261,5},{262,6},{263,7},{2... | collective-permute-start | bytes 393224 | tf_op jit(solution)/shard_map/ppermute | solution.py:14
  268.1 12.4 %collective-permute-start.22 = (f32[1,128,128]{1,2,0:T(8,128)}, f32[1,128,128]{1,2,0:T(8,128)}, u32[]{:S(2)}, u32[]{:S(2)}) collective-permute-start(f32[1,128,128]{1,2,0:T(8,128)} %fusion.88), channel_id=1, source_target_pairs={{0,64},{1,65},{2,66},{3,67},{4,68},{5,69},{6,70},{7,71},{8,72},{9,... | collective-permute-start | bytes 196616 | tf_op jit(solution)/shard_map/ppermute | solution.py:14
  281.6 10.1 %collective-permute-start.23 = (f32[1,128,128]{1,2,0:T(8,128)S(1)}, f32[1,128,128]{1,2,0:T(8,128)S(1)}, u32[]{:S(2)}, u32[]{:S(2)}) collective-permute-start(f32[1,128,128]{1,2,0:T(8,128)S(1)} %convolution_bitcast_fusion.7), channel_id=1, source_target_pairs={{64,0},{65,1},{66,2},{67,3},{68,4},{69,5},{70,6},{71,7},{72,8},{73... | collective-permute-start | bytes 196616 | tf_op jit(solution)/shard_map/ppermute | solution.py:14
  292.8 9.2 %collective-permute-start.24 = (f32[1,128,128]{1,2,0:T(8,128)S(1)}, f32[1,128,128]{1,2,0:T(8,128)S(1)}, u32[]{:S(2)}, u32[]{:S(2)}) collective-permute-start(f32[1,128,128]{1,2,0:T(8,128)S(1)} %fusion.89), channel_id=1, source_target_pairs={{0,32},{1,33},{2,34},{3,35},{4,36},{5,37},{6,38},{7,39},{8,40},{9,... | collective-permute-start | bytes 196616 | tf_op jit(solution)/shard_map/ppermute | solution.py:14
  310.9 8.4 %collective-permute-start.26 = (f32[1,128,128]{1,2,0:T(8,128)S(1)}, f32[1,128,128]{1,2,0:T(8,128)S(1)}, u32[]{:S(2)}, u32[]{:S(2)}) collective-permute-start(f32[1,128,128]{1,2,0:T(8,128)S(1)} %fusion.90), channel_id=1, source_target_pairs={{0,16},{1,17},{2,18},{3,19},{4,20},{5,21},{6,22},{7,23},{8,24},{9,... | collective-permute-start | bytes 196616 | tf_op jit(solution)/shard_map/ppermute | solution.py:14
  326.9 13.9 %collective-permute-start.28 = (f32[1,128,128]{1,2,0:T(8,128)S(1)}, f32[1,128,128]{1,2,0:T(8,128)S(1)}, u32[]{:S(2)}, u32[]{:S(2)}) collective-permute-start(f32[1,128,128]{1,2,0:T(8,128)S(1)} %fusion.91), channel_id=1, source_target_pairs={{0,8},{1,9},{2,10},{3,11},{4,12},{5,13},{6,14},{7,15},{8,16},{9,17... | collective-permute-start | bytes 196616 | tf_op jit(solution)/shard_map/ppermute | solution.py:14
  341.0 10.5 %collective-permute-start.29 = (f32[1,128,128]{1,2,0:T(8,128)S(1)}, f32[1,128,128]{1,2,0:T(8,128)S(1)}, u32[]{:S(2)}, u32[]{:S(2)}) collective-permute-start(f32[1,128,128]{1,2,0:T(8,128)S(1)} %convolution_bitcast_fusion.4), channel_id=1, source_target_pairs={{8,0},{9,1},{10,2},{11,3},{12,4},{13,5},{14,6},{15,7},{16,8},{17,9... | collective-permute-start | bytes 196616 | tf_op jit(solution)/shard_map/ppermute | solution.py:14
  352.5 11.3 %collective-permute-start.30 = (f32[1,128,128]{1,2,0:T(8,128)S(1)}, f32[1,128,128]{1,2,0:T(8,128)S(1)}, u32[]{:S(2)}, u32[]{:S(2)}) collective-permute-start(f32[1,128,128]{1,2,0:T(8,128)S(1)} %fusion.92), channel_id=1, source_target_pairs={{0,4},{1,5},{2,6},{3,7},{4,8},{5,9},{6,10},{7,11},{8,12},{9,13},{1... | collective-permute-start | bytes 196616 | tf_op jit(solution)/shard_map/ppermute | solution.py:14
  372.2 10.5 %collective-permute-start.32 = (f32[1,128,128]{1,2,0:T(8,128)S(1)}, f32[1,128,128]{1,2,0:T(8,128)S(1)}, u32[]{:S(2)}, u32[]{:S(2)}) collective-permute-start(f32[1,128,128]{1,2,0:T(8,128)S(1)} %fusion.93), channel_id=1, source_target_pairs={{0,2},{1,3},{2,4},{3,5},{4,6},{5,7},{6,8},{7,9},{8,10},{9,11},{10,... | collective-permute-start | bytes 196616 | tf_op jit(solution)/shard_map/ppermute | solution.py:14
  390.7 10.1 %collective-permute-start.34 = (f32[1,128,128]{1,2,0:T(8,128)}, f32[1,128,128]{1,2,0:T(8,128)S(1)}, u32[]{:S(2)}, u32[]{:S(2)}) collective-permute-start(f32[1,128,128]{1,2,0:T(8,128)} %fusion.94), channel_id=1, source_target_pairs={{0,1},{1,2},{2,3},{3,4},{4,5},{5,6},{6,7},{7,8},{8,9},{9,10},{10,1... | collective-permute-start | bytes 196616 | tf_op jit(solution)/shard_map/ppermute | solution.py:14
  (45 other events, 624.8 us)
where the time goes:
time: 437 us; the launch traced here: 434 us
  waiting for transfers between devices  177 us (41%)
  starting transfers between devices  96.1 us (22%)
  local copies, waits for them, and re-layouts  79.5 us (18%)
  matrix products  61.6 us (14%)
  other arithmetic  18 us (4%)
    ppermute x36, waiting for transfers between devices, shifted(): return lax.ppermute(block, axis, route)  177 us
    ppermute x36, starting transfers between devices, shifted(): return lax.ppermute(block, axis, route)  96.1 us
    gather x3, local copies, waits for them, and re-layouts, arrange(): source = tree_order[jnp.clip(position, 0, point_count - 1)]  23 us
    gather x2, local copies, waits for them, and re-layouts, arrange(): values[source]  16.5 us
    dot_general x13, matrix products, climb(): jnp.einsum('jkq,jkr->jqr', coupling, left_part, precision=exact_products)  15.7 us
    gather x1, local copies, waits for them, and re-layouts, arrange(): leaf_points = points[:, source]  15.6 us
    scatter x1, local copies, waits for them, and re-layouts, body(): result = jnp.zeros((values.shape[0], rhs_width), jnp.float32).at[target.r...  11.3 us
    dot_general x13, matrix products, climb(): jnp.einsum('jqk,jkr->jqr', coupling, right_part, precision=exact_products)  9.71 us
  transfers between devices with their start and end apart: 36, of which 31 were waited for; matrix products, arithmetic and copies ran while one was open for 15% of the time, Pallas kernels for 0%

commit v1 on v0

v1 whole, which is shorter than its diff:
```python
import functools

import jax
import jax.numpy as jnp
from jax import lax
from jax.experimental import pallas as pl
from jax.experimental.pallas import tpu as pltpu
from jax.sharding import PartitionSpec as P

F32 = jnp.float32
BF16 = jnp.bfloat16
MESH = pl.DeviceIdType.MESH
VMEM = pl.BlockSpec(memory_space=pltpu.VMEM)
SMEM = pl.BlockSpec(memory_space=pltpu.SMEM)
VMEM_LIMIT = 56 * 2**20

PTS = 3072
LEAF = 256
LEAVES = 16
R = 128
UNROLL = 32


def point_pieces(p):
    h = p.astype(BF16).astype(F32)
    rest = p - h
    m = rest.astype(BF16).astype(F32)
    low = (rest - m).astype(BF16).astype(F32)
    q = jnp.sum(p * p, axis=0, keepdims=True) * -0.125
    qh = q.astype(BF16).astype(F32)
    rest = q - qh
    qm = rest.astype(BF16).astype(F32)
    ql = (rest - qm).astype(BF16).astype(F32)
    n = p.shape[1]
    row = lax.broadcasted_iota(jnp.int32, (8, n), 0)
    parts = jnp.where(row % 3 == 0, qh, jnp.where(row % 3 == 1, qm, ql))
    left_q = jnp.where(row < 3, parts, jnp.where(row < 6, 1.0, 0.0))
    right_q = jnp.where(row < 3, 1.0, jnp.where(row < 6, parts, 0.0))
    zero = jnp.zeros((8, n), F32)
    left = [h * 0.25, h * 0.25, m * 0.25, m * 0.25, h * 0.25, low * 0.25, left_q, zero]
    right = [h, m, h, m, low, h, right_q, zero]
    return jnp.concatenate(left + right, axis=0)


def gather_kernel(order, sizes, v_ref, p_ref, rows_out, pts_out, tv, tp, gv, gp):
    tv[...] = v_ref[...].astype(F32)
    for c in range(PTS // 128):
        span = slice(128 * c, 128 * (c + 1))
        tp[span, :] = point_pieces(p_ref[:, span]).T
    gv[PTS:, :] = jnp.zeros((LEAF, R), F32)
    gp[PTS:, :] = jnp.zeros((LEAF, R), F32)

    def move(i, carry):
        base = pl.multiple_of(i * UNROLL, UNROLL)
        for u in range(UNROLL):
            source = order[0, base + u]
            gv[pl.ds(base + u, 1), :] = tv[pl.ds(source, 1), :]
            gp[pl.ds(base + u, 1), :] = tp[pl.ds(source, 1), :]
        return carry

    lax.fori_loop(0, PTS // UNROLL, move, 0)
    slot = lax.broadcasted_iota(jnp.int32, (LEAF, R), 0)
    start = 0
    for t in range(LEAVES):
        size = sizes[0, t]
        rows = gv[pl.ds(start, LEAF), :]
        rows_out[t] = jnp.where(slot < size, rows, 0.0).astype(BF16)
        pts_out[t] = gp[pl.ds(start, LEAF), :].astype(BF16)
        start = start + size


def gather(values, points, order, sizes):
    return pl.pallas_call(
        gather_kernel,
        out_shape=[
            jax.ShapeDtypeStruct((LEAVES, LEAF, R), BF16),
            jax.ShapeDtypeStruct((LEAVES, LEAF, R), BF16),
        ],
        in_specs=[SMEM, SMEM, VMEM, VMEM],
        out_specs=[VMEM, VMEM],
        scratch_shapes=[
            pltpu.VMEM((PTS, R), F32),
            pltpu.VMEM((PTS, R), F32),
            pltpu.VMEM((PTS + LEAF, R), F32),
            pltpu.VMEM((PTS + LEAF, R), F32),
        ],
        compiler_params=pltpu.CompilerParams(vmem_limit_bytes=VMEM_LIMIT),
        name="gather_rows",
    )(order, sizes, values, points)


def scatter_kernel(order, sizes, total, out, tree, held):
    start = 0
    for t in range(LEAVES):
        tree[pl.ds(start, LEAF), :] = total[t].astype(F32)
        start = start + sizes[0, t]

    def move(i, carry):
        base = pl.multiple_of(i * UNROLL, UNROLL)
        for u in range(UNROLL):
            held[pl.ds(order[0, base + u], 1), :] = tree[pl.ds(base + u, 1), :]
        return carry

    lax.fori_loop(0, PTS // UNROLL, move, 0)
    out[...] = held[...].astype(BF16)


def scatter(total, order, sizes):
    return pl.pallas_call(
        scatter_kernel,
        out_shape=jax.ShapeDtypeStruct((PTS, R), BF16),
        in_specs=[SMEM, SMEM, VMEM],
        out_specs=VMEM,
        scratch_shapes=[
            pltpu.VMEM((PTS + LEAF, R), F32),
            pltpu.VMEM((PTS, R), F32),
        ],
        compiler_params=pltpu.CompilerParams(vmem_limit_bytes=VMEM_LIMIT),
        name="scatter_rows",
    )(order, sizes, total)


def dot(a, b, ca=1, cb=0):
    return lax.dot_general(a, b, (((ca,), (cb,)), ((), ())), preferred_element_type=F32)


def split(x):
    h = x.astype(BF16)
    return jnp.concatenate([h, (x - h.astype(F32)).astype(BF16)], axis=0)


def mm(x, w):
    y = dot(split(x), w)
    return y[: x.shape[0]] + y[x.shape[0] :]


def mmt(x, w):
    y = dot(split(x), w, 1, 1)
    return y[: x.shape[0]] + y[x.shape[0] :]


def flip(v, m):
    out = v
    for i in range(3):
        if (m >> i) & 1:
            bit = lax.rem(lax.div(v, 2**i), 2)
            out = out + (1 - 2 * bit) * 2**i
    return out


def reach(m):
    return m.bit_length() - 1


def tree_kernel(
    rows, pts, basis, transfer, coupling, ctrans, ccoup, total,
    coef, term, field, near, own, core_mats, core_coef, up_field,
    path, piece, xpiece, zlev, xlev, mat_w, mat_c,
    prod, yslice, yblock, zsend, zgot, xsend, xgot, gdown, fdown,
    s_core, r_core, s_dir, r_dir, s_m1, r_m1, s_m2, r_m2, s_m3, r_m3, s_m4, r_m4, s_m5, r_m5,
    s_ys, r_ys, s_yb, r_yb, s_z, r_z, s_x, r_x, s_yd, r_yd,
):
    me = lax.axis_index("leaf")
    core = lax.rem(me, 2)
    y = lax.rem(lax.div(me, 2), 8)
    z = lax.rem(lax.div(me, 16), 8)
    x = lax.div(me, 128)
    is0 = core == 0
    is1 = core == 1

    def at(xx, zz, yy):
        return ((xx * 8 + zz) * 8 + yy) * 2

    mate = me + 1 - 2 * core
    along_y = [at(x, z, flip(y, m)) for m in range(8)]
    along_z = [at(x, flip(z, m), y) for m in range(8)]
    along_x = [at(flip(x, m), z, y) for m in range(4)]

    def copy(src, dst, send, recv, to):
        return pltpu.make_async_remote_copy(
            src_ref=src, dst_ref=dst, send_sem=send, recv_sem=recv, device_id=(to,), device_id_type=MESH
        )

    own[0] = ctrans[0, 0].astype(F32)
    own[1] = ccoup[0].astype(F32)
    own[2] = ctrans[0, 1].astype(F32)

    barrier = pltpu.get_barrier_semaphore()
    pl.semaphore_signal(barrier, inc=1, device_id=(mate,), device_id_type=MESH)

    @pl.when(is0)
    def _():
        for to in along_y[1:] + along_z[1:] + along_x[1:]:
            pl.semaphore_signal(barrier, inc=1, device_id=(to,), device_id_type=MESH)
        pl.semaphore_wait(barrier, 18)

    @pl.when(is1)
    def _():
        pl.semaphore_wait(barrier, 1)

    def c_mats():
        return copy(own, core_mats, s_core.at[0], r_core.at[0], mate)

    def c_coef():
        return copy(coef.at[30], core_coef, s_core.at[1], r_core.at[1], mate)

    def c_field():
        return copy(up_field, up_field, s_core.at[2], r_core.at[2], mate)


    def direct(level, i):
        size = 2 << level
        half = size // 2
        src = own.at[0:2] if i < half else own.at[1:3]
        return copy(src, path.at[level], s_dir.at[i], r_dir.at[level], at(x, z, y - half + i))

    def direct_all(level):
        size = 2 << level
        return [direct(level, i) for i in range(size) if i != size // 2]

    def m1(k):
        return copy(own.at[:, 16 * k : 16 * k + 16, :], piece.at[z], s_m1.at[k], r_m1, at(x, z, k))

    def m2(m):
        return copy(piece.at[z], piece.at[z], s_m2.at[m], r_m2.at[m], along_z[m])

    def m2_from(m):
        there = piece.at[flip(z, m)]
        return copy(there, there, s_m2.at[m], r_m2.at[m], along_z[m])

    def m3(m):
        return copy(piece.at[0], xpiece.at[x], s_m3.at[m], r_m3.at[m], along_x[m])

    def m3_from(m):
        return copy(piece.at[0], xpiece.at[flip(x, m)], s_m3.at[m], r_m3.at[m], along_x[m])

    def m4(m):
        return copy(zlev.at[y], zlev.at[y], s_m4.at[m], r_m4.at[m], along_y[m])

    def m4_from(m):
        return copy(zlev.at[y], zlev.at[flip(y, m)], s_m4.at[m], r_m4.at[m], along_y[m])

    def m5(m):
        return copy(xlev.at[y], xlev.at[y], s_m5.at[m], r_m5.at[m], along_y[m])

    def m5_from(m):
        return copy(xlev.at[y], xlev.at[flip(y, m)], s_m5.at[m], r_m5.at[m], along_y[m])

    def ys(m):
        part = prod.at[3, pl.ds(pl.multiple_of(16 * flip(y, m), 16), 16), :]
        return copy(part, yslice.at[m], s_ys.at[m], r_ys.at[m], along_y[m])

    def yb(m):
        return copy(prod.at[reach(m)], yblock.at[m], s_yb.at[m], r_yb.at[m], along_y[m])

    def zs(m):
        return copy(zsend.at[reach(m)], zgot.at[m], s_z.at[m], r_z.at[m], along_z[m])

    def xs(m):
        return copy(xsend.at[reach(m)], xgot.at[m], s_x.at[m], r_x.at[m], along_x[m])

    def yd(m):
        return copy(gdown, fdown.at[y], s_yd.at[m], r_yd.at[m], along_y[m])

    def yd_from(m):
        return copy(gdown, fdown.at[flip(y, m)], s_yd.at[m], r_yd.at[m], along_y[m])

    @pl.when(is1)
    def _():
        c_mats().start()
        core_mats[...] = own[...]

    @pl.when(is0)
    def _():
        @pl.when(y == 0)
        def _():
            for k in range(1, 8):
                m1(k).start()
            piece[z] = own[:, 0:16, :]

        for level in range(3):
            size = 2 << level

            @pl.when(lax.rem(y, size) == size // 2)
            def _():
                for c in direct_all(level):
                    c.start()
                path[level] = own[1:3]

    def leaf(t, carry):
        coef[t] = dot(rows[t], basis[t], 0, 0)
        return carry

    lax.fori_loop(0, LEAVES, leaf, 0, unroll=4)

    eye = (
        lax.broadcasted_iota(jnp.int32, (LEAF, LEAF), 0) == lax.broadcasted_iota(jnp.int32, (LEAF, LEAF), 1)
    ).astype(F32)
    shift = (
        lax.broadcasted_iota(jnp.int32, (R, R), 0) == lax.broadcasted_iota(jnp.int32, (R, R), 1) + 64
    ).astype(F32).astype(BF16)

    def nearby(t, carry):
        left = pts[t]
        right = dot(left, shift).astype(BF16)
        kernel = (jnp.exp(dot(left, right, 1, 1)) + eye).astype(BF16)
        near[t] = dot(kernel, rows[t])
        return carry

    lax.fori_loop(0, 8, nearby, 0, unroll=2)

    @pl.when(is0)
    def _():
        @pl.when(y > 0)
        def _():
            m1(1).wait_recv()

        for m in range(1, 8):
            m2(m).start()

    def climb(j, carry):
        both = jnp.concatenate([coef[2 * j], coef[2 * j + 1]], axis=1)
        coef[16 + j] = mm(both, transfer[j])
        return carry

    lax.fori_loop(0, 8, climb, 0, unroll=4)
    lax.fori_loop(8, 12, climb, 0, unroll=4)
    lax.fori_loop(12, 14, climb, 0, unroll=2)
    climb(14, 0)
    c_coef().start()

    def terms(j, carry):
        term[2 * j] = mmt(coef[2 * j + 1], coupling[j])
        term[2 * j + 1] = mm(coef[2 * j], coupling[j])
        return carry

    lax.fori_loop(0, 15, terms, 0, unroll=3)
    c_coef().wait()

    @pl.when(is0)
    def _():
        for level in range(3):
            size = 2 << level

            @pl.when(lax.rem(y, size) != size // 2)
            def _():
                copy(own.at[0:2], path.at[level], s_dir.at[0], r_dir.at[level], mate).wait_recv()

            side = lax.rem(lax.div(y, size // 2), 2)
            mat_w[level] = path[level, side].astype(BF16)
            c = path[level, 1 - side]
            mat_c[level] = jnp.where(side == 0, c.T, c).astype(BF16)

        c_mats().wait_recv()
        pair = jnp.concatenate([core_mats[0], core_mats[2]], axis=0).astype(BF16)
        prod[0] = mm(jnp.concatenate([coef[30], core_coef[...]], axis=1), pair)
        for level in range(3):
            prod[level + 1] = mm(prod[level], mat_w[level])
        for m in range(1, 8):
            ys(m).start()
        yslice[0] = prod[3, pl.ds(pl.multiple_of(16 * y, 16), 16), :]

        for m in range(1, 8):
            m2_from(m).wait_recv()
        for m in range(1, 4):
            m3(m).start()
        xpiece[x] = piece[0]
        for i in range(3):
            half = 1 << i
            owner = lax.div(z, 2 * half) * 2 * half + half
            side = lax.rem(lax.div(z, half), 2)
            zlev[y, 2 * i] = piece[owner, 2 * side]
            zlev[y, 2 * i + 1] = piece[owner, 1]
        for m in range(1, 8):
            m4(m).start()
        for m in range(1, 4):
            m3_from(m).wait_recv()
        owner = lax.div(x, 2) * 2 + 1
        xlev[y, 0] = xpiece[owner, 2 * lax.rem(x, 2)]
        xlev[y, 1] = xpiece[owner, 1]
        xlev[y, 2] = xpiece[2, 1]
        for m in range(1, 8):
            m5(m).start()
        for m in range(1, 8):
            yb(m).start()

    lax.fori_loop(8, LEAVES, nearby, 0, unroll=2)

    @pl.when(is0)
    def _():
        for m in range(1, 8):
            m4_from(m).wait_recv()
        for i in range(3):
            mat_w[3 + i] = zlev[:, 2 * i].reshape(R, R).astype(BF16)
            c = zlev[:, 2 * i + 1].reshape(R, R)
            mat_c[3 + i] = jnp.where(lax.rem(lax.div(z, 1 << i), 2) == 0, c.T, c).astype(BF16)
        for m in range(1, 8):
            ys(m).wait_recv()
        u = yslice[0]
        for m in range(1, 8):
            u = u + yslice[m]
        for i in range(3):
            zsend[i, 0] = u
            u = mm(u, mat_w[3 + i])
        for i in range(3):
            zsend[i, 1] = u
        for m in range(1, 8):
            zs(m).start()

        for m in range(1, 8):
            m5_from(m).wait_recv()
        mat_w[6] = xlev[:, 0].reshape(R, R).astype(BF16)
        c = xlev[:, 1].reshape(R, R)
        mat_c[6] = jnp.where(lax.rem(x, 2) == 0, c.T, c).astype(BF16)
        c = xlev[:, 2].reshape(R, R)
        mat_c[7] = jnp.where(lax.div(x, 2) == 0, c.T, c).astype(BF16)

        for m in range(1, 8):
            zs(m).wait_recv()
            u = u + zgot[m, 1]
        xsend[0] = u
        xsend[1] = mm(u, mat_w[6])
        for m in range(1, 4):
            xs(m).start()
        side_z = [
            mm(zgot[1, 0], mat_c[3]),
            mm(zgot[2, 0] + zgot[3, 0], mat_c[4]),
            mm((zgot[4, 0] + zgot[5, 0]) + (zgot[6, 0] + zgot[7, 0]), mat_c[5]),
        ]
        for m in range(1, 4):
            xs(m).wait_recv()
        g = mm(xgot[2] + xgot[3], mat_c[7])
        g = mmt(g, mat_w[6]) + mm(xgot[1], mat_c[6])
        for i in (2, 1, 0):
            g = mmt(g, mat_w[3 + i]) + side_z[i]
        gdown[...] = g
        for m in range(1, 8):
            yd(m).start()
        fdown[y] = g

        for m in range(1, 8):
            yb(m).wait_recv()
        side_y = [
            mm(yblock[1], mat_c[0]),
            mm(yblock[2] + yblock[3], mat_c[1]),
            mm((yblock[4] + yblock[5]) + (yblock[6] + yblock[7]), mat_c[2]),
        ]
        for m in range(1, 8):
            yd_from(m).wait_recv()
        f = fdown[...].reshape(R, R)
        for level in (2, 1, 0):
            f = mmt(f, mat_w[level]) + side_y[level]
        up_field[...] = f
        c_field().start()

    @pl.when(is1)
    def _():
        c_field().wait_recv()

    weight = jnp.where(is0, core_mats[0], core_mats[2]).astype(BF16)
    c = core_mats[1]
    across = jnp.where(is0, c.T, c).astype(BF16)
    field[30] = mmt(up_field[...], weight) + mm(core_coef[...], across)

    def descend(i, carry):
        j = 14 - i
        both = mmt(field[16 + j], transfer[j])
        field[2 * j] = both[:, :R] + term[2 * j]
        field[2 * j + 1] = both[:, R:] + term[2 * j + 1]
        return carry

    descend(0, 0)
    lax.fori_loop(1, 3, descend, 0, unroll=2)
    lax.fori_loop(3, 7, descend, 0, unroll=4)
    lax.fori_loop(7, 15, descend, 0, unroll=4)

    def finish(t, carry):
        total[t] = (near[t] + dot(basis[t], field[t].astype(BF16), 1, 1)).astype(BF16)
        return carry

    lax.fori_loop(0, LEAVES, finish, 0, unroll=4)

    @pl.when(is1)
    def _():
        c_mats().wait_send()

    @pl.when(is0)
    def _():
        c_field().wait_send()

        @pl.when(y == 0)
        def _():
            for k in range(1, 8):
                m1(k).wait_send()

        for level in range(3):
            size = 2 << level

            @pl.when(lax.rem(y, size) == size // 2)
            def _():
                for c in direct_all(level):
                    c.wait_send()

        for m in range(1, 8):
            for group in (m2, m4, m5, ys, yb, zs, yd):
                group(m).wait_send()
        for m in range(1, 4):
            for group in (m3, xs):
                group(m).wait_send()


def tree(rows, pts, basis, transfer, coupling, ctrans, ccoup):
    dma = pltpu.SemaphoreType.DMA
    block = (R, R)
    return pl.pallas_call(
        tree_kernel,
        out_shape=jax.ShapeDtypeStruct((LEAVES, LEAF, R), BF16),
        in_specs=[VMEM] * 7,
        out_specs=VMEM,
        scratch_shapes=[
            pltpu.VMEM((31,) + block, F32),
            pltpu.VMEM((30,) + block, F32),
            pltpu.VMEM((31,) + block, F32),
            pltpu.VMEM((LEAVES, LEAF, R), F32),
            pltpu.VMEM((3,) + block, F32),
            pltpu.VMEM((3,) + block, F32),
            pltpu.VMEM(block, F32),
            pltpu.VMEM(block, F32),
            pltpu.VMEM((3, 2) + block, F32),
            pltpu.VMEM((8, 3, 16, R), F32),
            pltpu.VMEM((4, 3, 16, R), F32),
            pltpu.VMEM((8, 6, 16, R), F32),
            pltpu.VMEM((8, 3, 16, R), F32),
            pltpu.VMEM((7,) + block, BF16),
            pltpu.VMEM((8,) + block, BF16),
            pltpu.VMEM((4,) + block, F32),
            pltpu.VMEM((8, 16, R), F32),
            pltpu.VMEM((8,) + block, F32),
            pltpu.VMEM((3, 2, 16, R), F32),
            pltpu.VMEM((8, 2, 16, R), F32),
            pltpu.VMEM((2, 16, R), F32),
            pltpu.VMEM((4, 16, R), F32),
            pltpu.VMEM((16, R), F32),
            pltpu.VMEM((8, 16, R), F32),
            dma((3,)), dma((3,)),
            dma((8,)), dma((3,)),
            dma((8,)), dma,
            dma((8,)), dma((8,)),
            dma((4,)), dma((4,)),
            dma((8,)), dma((8,)),
            dma((8,)), dma((8,)),
            dma((8,)), dma((8,)),
            dma((8,)), dma((8,)),
            dma((8,)), dma((8,)),
            dma((4,)), dma((4,)),
            dma((8,)), dma((8,)),
        ],
        compiler_params=pltpu.CompilerParams(
            collective_id=0, has_side_effects=True, vmem_limit_bytes=VMEM_LIMIT
        ),
        name="tree",
    )(rows, pts, basis, transfer, coupling, ctrans, ccoup)


def body(
    values,
    points,
    tree_order,
    leaf_sizes,
    leaf_basis,
    local_transfer,
    local_coupling,
    cross_transfer,
    cross_coupling,
):
    rows, pts = gather(values, points, tree_order, leaf_sizes)
    transfer = local_transfer.reshape(LEAVES - 1, 2 * R, R)
    total = tree(rows, pts, leaf_basis, transfer, local_coupling, cross_transfer, cross_coupling)
    return scatter(total, tree_order, leaf_sizes)


def solution(mesh):
    in_specs = (
        P("leaf", None),
        P(None, "leaf"),
        P("leaf", None),
        P("leaf", None),
        P("leaf", None, None),
        P("leaf", None, None, None),
        P("leaf", None, None),
        P("leaf", None, None, None),
        P("leaf", None, None),
    )
    out_specs = P("leaf", None)
    return jax.shard_map(body, mesh=mesh, in_specs=in_specs, out_specs=out_specs, check_vma=False)
```

time: 437 us -> 70.8 us (0.16)
  the two profiles are of different devices: /device:TPU:2 before, /device:TPU:1 now
where the time goes in v1:
time: 70.8 us; the launch traced here: 70.5 us
  Pallas kernels  70.5 us (100%)
    pallas_call x1, Pallas kernels, tree(): pl.pallas_call(tree_kernel, out_shape=jax.ShapeDtypeStruct((LEAVES, LEAF,...  58.3 us
    pallas_call x1, Pallas kernels, gather(): pl.pallas_call(gather_kernel, out_shape=[jax.ShapeDtypeStruct((LEAVES, LE...  6.99 us
    pallas_call x1, Pallas kernels, scatter(): pl.pallas_call(scatter_kernel, out_shape=jax.ShapeDtypeStruct((PTS, R), B...  5.21 us

profile of v1, /device:TPU:1, one launch (start us, length us, event | category | flops | bytes accessed | tf_op | source)
XLA Modules:
  0.0 70.5 jit_solution(18059461711745726408)
XLA Ops:
  0.0 7.0 %gather_rows.1 = (bf16[16,256,128]{2,1,0:T(8,128)(2,1)}, bf16[16,256,128]{2,1,0:T(8,128)(2,1)}) custom-call(s32[1,3072]{1,0:T(1,128)} %order.3, s32[1,16]{1,0:T(1,128)} %sizes.3, bf16[3072,128]{1,0:T(8,128)(2,1)} %v_ref.1, f32[8,3072]{1,0:T(8,128)} %p_ref.1), custom_call_target="tpu_custom_call" | custom-call | tf_op jit(solution)/shard_map/gather_rows/pallas_call | solution.py:73
  7.0 58.3 %tree.1.total = bf16[16,256,128]{2,1,0:T(8,128)(2,1)} custom-call(bf16[16,256,128]{2,1,0:T(8,128)(2,1)} %get-tuple-element.7.rows, bf16[16,256,128]{2,1,0:T(8,128)(2,1)} %get-tuple-element.8.pts, bf16[16,256,128]{2,1,0:T(8,128)(2,1)} %basis.1, bf16[15,256,128]{2,1,0:T(8,128)(2,1)} %bitcast.1, bf16[15,128,128]{2,1,0:T(8,128)(2,1)} %coupling.1, ...), custom_call_target="tpu_custom_call" | custom-call | tf_op jit(solution)/shard_map/tree/pallas_call | solution.py:515
  65.3 5.2 %scatter_rows.1 = bf16[3072,128]{1,0:T(8,128)(2,1)} custom-call(s32[1,3072]{1,0:T(1,128)} %order.3, s32[1,16]{1,0:T(1,128)} %sizes.3, bf16[16,256,128]{2,1,0:T(8,128)(2,1)} %tree.1.total), custom_call_target="tpu_custom_call" | custom-call | tf_op jit(solution)/shard_map/scatter_rows/pallas_call | solution.py:109

commit v2 on v1

--- a/solution.py
+++ b/solution.py
@@ -12,6 +12,7 @@
 MESH = pl.DeviceIdType.MESH
 VMEM = pl.BlockSpec(memory_space=pltpu.VMEM)
 SMEM = pl.BlockSpec(memory_space=pltpu.SMEM)
+HBM = pl.BlockSpec(memory_space=pl.ANY)
 VMEM_LIMIT = 56 * 2**20
 
 PTS = 3072
@@ -42,53 +43,6 @@
     return jnp.concatenate(left + right, axis=0)
 
 
-def gather_kernel(order, sizes, v_ref, p_ref, rows_out, pts_out, tv, tp, gv, gp):
-    tv[...] = v_ref[...].astype(F32)
-    for c in range(PTS // 128):
-        span = slice(128 * c, 128 * (c + 1))
-        tp[span, :] = point_pieces(p_ref[:, span]).T
-    gv[PTS:, :] = jnp.zeros((LEAF, R), F32)
-    gp[PTS:, :] = jnp.zeros((LEAF, R), F32)
-
-    def move(i, carry):
-        base = pl.multiple_of(i * UNROLL, UNROLL)
-        for u in range(UNROLL):
-            source = order[0, base + u]
-            gv[pl.ds(base + u, 1), :] = tv[pl.ds(source, 1), :]
-            gp[pl.ds(base + u, 1), :] = tp[pl.ds(source, 1), :]
-        return carry
-
-    lax.fori_loop(0, PTS // UNROLL, move, 0)
-    slot = lax.broadcasted_iota(jnp.int32, (LEAF, R), 0)
-    start = 0
-    for t in range(LEAVES):
-        size = sizes[0, t]
-        rows = gv[pl.ds(start, LEAF), :]
-        rows_out[t] = jnp.where(slot < size, rows, 0.0).astype(BF16)
-        pts_out[t] = gp[pl.ds(start, LEAF), :].astype(BF16)
-        start = start + size
-
-
-def gather(values, points, order, sizes):
-    return pl.pallas_call(
-        gather_kernel,
-        out_shape=[
-            jax.ShapeDtypeStruct((LEAVES, LEAF, R), BF16),
-            jax.ShapeDtypeStruct((LEAVES, LEAF, R), BF16),
-        ],
-        in_specs=[SMEM, SMEM, VMEM, VMEM],
-        out_specs=[VMEM, VMEM],
-        scratch_shapes=[
-            pltpu.VMEM((PTS, R), F32),
-            pltpu.VMEM((PTS, R), F32),
-            pltpu.VMEM((PTS + LEAF, R), F32),
-            pltpu.VMEM((PTS + LEAF, R), F32),
-        ],
-        compiler_params=pltpu.CompilerParams(vmem_limit_bytes=VMEM_LIMIT),
-        name="gather_rows",
-    )(order, sizes, values, points)
-
-
 def scatter_kernel(order, sizes, total, out, tree, held):
     start = 0
     for t in range(LEAVES):
@@ -153,7 +107,8 @@
 
 
 def tree_kernel(
-    rows, pts, basis, transfer, coupling, ctrans, ccoup, total,
+    order, sizes, v_ref, p_ref, basis_any, transfer_any, coupling_any, ctrans, ccoup, total,
+    basis, transfer, coupling, s_local, tv, tp, gv, gp, rows, pts,
     coef, term, field, near, own, core_mats, core_coef, up_field,
     path, piece, xpiece, zlev, xlev, mat_w, mat_c,
     prod, yslice, yblock, zsend, zgot, xsend, xgot, gdown, fdown,
@@ -181,6 +136,15 @@
             src_ref=src, dst_ref=dst, send_sem=send, recv_sem=recv, device_id=(to,), device_id_type=MESH
         )
 
+    loads = [
+        pltpu.make_async_copy(src, dst, s_local.at[i])
+        for i, (src, dst) in enumerate(
+            [(basis_any, basis), (transfer_any, transfer), (coupling_any, coupling)]
+        )
+    ]
+    for load in loads:
+        load.start()
+
     own[0] = ctrans[0, 0].astype(F32)
     own[1] = ccoup[0].astype(F32)
     own[2] = ctrans[0, 1].astype(F32)
@@ -192,6 +156,13 @@
     def _():
         for to in along_y[1:] + along_z[1:] + along_x[1:]:
             pl.semaphore_signal(barrier, inc=1, device_id=(to,), device_id_type=MESH)
+
+    tv[...] = v_ref[...].astype(F32)
+    gv[PTS:, :] = jnp.zeros((LEAF, R), F32)
+    gp[PTS:, :] = jnp.zeros((LEAF, R), F32)
+
+    @pl.when(is0)
+    def _():
         pl.semaphore_wait(barrier, 18)
 
     @pl.when(is1)
@@ -208,15 +179,16 @@
         return copy(up_field, up_field, s_core.at[2], r_core.at[2], mate)
 
 
-    def direct(level, i):
+    def direct(level, i, which):
         size = 2 << level
         half = size // 2
-        src = own.at[0:2] if i < half else own.at[1:3]
-        return copy(src, path.at[level], s_dir.at[i], r_dir.at[level], at(x, z, y - half + i))
+        src = own.at[1] if which else own.at[0 if i < half else 2]
+        to = at(x, z, y - half + i)
+        return copy(src, path.at[level, which], s_dir.at[which, i], r_dir.at[which, level], to)
 
     def direct_all(level):
         size = 2 << level
-        return [direct(level, i) for i in range(size) if i != size // 2]
+        return [direct(level, i, which) for which in range(2) for i in range(size) if i != size // 2]
 
     def m1(k):
         return copy(own.at[:, 16 * k : 16 * k + 16, :], piece.at[z], s_m1.at[k], r_m1, at(x, z, k))
@@ -285,29 +257,19 @@
             def _():
                 for c in direct_all(level):
                     c.start()
-                path[level] = own[1:3]
-
-    def leaf(t, carry):
-        coef[t] = dot(rows[t], basis[t], 0, 0)
-        return carry
-
-    lax.fori_loop(0, LEAVES, leaf, 0, unroll=4)
-
-    eye = (
-        lax.broadcasted_iota(jnp.int32, (LEAF, LEAF), 0) == lax.broadcasted_iota(jnp.int32, (LEAF, LEAF), 1)
-    ).astype(F32)
-    shift = (
-        lax.broadcasted_iota(jnp.int32, (R, R), 0) == lax.broadcasted_iota(jnp.int32, (R, R), 1) + 64
-    ).astype(F32).astype(BF16)
-
-    def nearby(t, carry):
-        left = pts[t]
-        right = dot(left, shift).astype(BF16)
-        kernel = (jnp.exp(dot(left, right, 1, 1)) + eye).astype(BF16)
-        near[t] = dot(kernel, rows[t])
-        return carry
-
-    lax.fori_loop(0, 8, nearby, 0, unroll=2)
+                path[level, 0] = own[2]
+                path[level, 1] = own[1]
+
+    def permute(table, placed, first, last):
+        def move(i, carry):
+            base = pl.multiple_of(i * UNROLL, UNROLL)
+            for u in range(UNROLL):
+                placed[pl.ds(base + u, 1), :] = table[pl.ds(order[0, base + u], 1), :]
+            return carry
+
+        lax.fori_loop(first // UNROLL, last // UNROLL, move, 0)
+
+    permute(tv, gv, 0, PTS)
 
     @pl.when(is0)
     def _():
@@ -318,48 +280,65 @@
         for m in range(1, 8):
             m2(m).start()
 
-    def climb(j, carry):
+    slot = lax.broadcasted_iota(jnp.int32, (LEAF, R), 0)
+    starts = [0]
+    for t in range(LEAVES):
+        size = sizes[0, t]
+        rows[t] = jnp.where(slot < size, gv[pl.ds(starts[t], LEAF), :], 0.0).astype(BF16)
+        starts.append(starts[t] + size)
+    loads[0].wait()
+    for t in range(LEAVES):
+        coef[t] = dot(rows[t], basis[t], 0, 0)
+    loads[1].wait()
+    for j in range(15):
         both = jnp.concatenate([coef[2 * j], coef[2 * j + 1]], axis=1)
         coef[16 + j] = mm(both, transfer[j])
-        return carry
-
-    lax.fori_loop(0, 8, climb, 0, unroll=4)
-    lax.fori_loop(8, 12, climb, 0, unroll=4)
-    lax.fori_loop(12, 14, climb, 0, unroll=2)
-    climb(14, 0)
     c_coef().start()
 
-    def terms(j, carry):
+    loads[2].wait()
+    for j in range(15):
         term[2 * j] = mmt(coef[2 * j + 1], coupling[j])
         term[2 * j + 1] = mm(coef[2 * j], coupling[j])
-        return carry
-
-    lax.fori_loop(0, 15, terms, 0, unroll=3)
-    c_coef().wait()
-
-    @pl.when(is0)
-    def _():
+
+    @pl.when(is0)
+    def _():
+        for which in range(2):
+            for level in range(3):
+                size = 2 << level
+
+                @pl.when(lax.rem(y, size) != size // 2)
+                def _():
+                    copy(
+                        own.at[0], path.at[level, which], s_dir.at[0, 0], r_dir.at[which, level], mate
+                    ).wait_recv()
+
+                if which == 0:
+                    mat_w[level] = path[level, 0].astype(BF16)
+            if which == 0:
+                c_mats().wait_recv()
+                c_coef().wait()
+                pair = jnp.concatenate([core_mats[0], core_mats[2]], axis=0).astype(BF16)
+                prod[0] = mm(jnp.concatenate([coef[30], core_coef[...]], axis=1), pair)
+                for level in range(3):
+                    prod[level + 1] = mm(prod[level], mat_w[level])
+                for m in range(1, 8):
+                    ys(m).start()
+                yslice[0] = prod[3, pl.ds(pl.multiple_of(16 * y, 16), 16), :]
         for level in range(3):
-            size = 2 << level
-
-            @pl.when(lax.rem(y, size) != size // 2)
-            def _():
-                copy(own.at[0:2], path.at[level], s_dir.at[0], r_dir.at[level], mate).wait_recv()
-
-            side = lax.rem(lax.div(y, size // 2), 2)
-            mat_w[level] = path[level, side].astype(BF16)
-            c = path[level, 1 - side]
-            mat_c[level] = jnp.where(side == 0, c.T, c).astype(BF16)
-
-        c_mats().wait_recv()
-        pair = jnp.concatenate([core_mats[0], core_mats[2]], axis=0).astype(BF16)
-        prod[0] = mm(jnp.concatenate([coef[30], core_coef[...]], axis=1), pair)
-        for level in range(3):
-            prod[level + 1] = mm(prod[level], mat_w[level])
-        for m in range(1, 8):
-            ys(m).start()
-        yslice[0] = prod[3, pl.ds(pl.multiple_of(16 * y, 16), 16), :]
-
+            c = path[level, 1]
+            mat_c[level] = jnp.where(lax.rem(lax.div(y, 1 << level), 2) == 0, c.T, c).astype(BF16)
+
+    @pl.when(is1)
+    def _():
+        c_coef().wait()
+
+    for c in range(PTS // 128):
+        span = slice(128 * c, 128 * (c + 1))
+        tp[span, :] = point_pieces(p_ref[:, span]).T
+    permute(tp, gp, 0, PTS // 4)
+
+    @pl.when(is0)
+    def _():
         for m in range(1, 8):
             m2_from(m).wait_recv()
         for m in range(1, 4):
@@ -373,6 +352,11 @@
             zlev[y, 2 * i + 1] = piece[owner, 1]
         for m in range(1, 8):
             m4(m).start()
+
+    permute(tp, gp, PTS // 4, PTS)
+
+    @pl.when(is0)
+    def _():
         for m in range(1, 4):
             m3_from(m).wait_recv()
         owner = lax.div(x, 2) * 2 + 1
@@ -384,7 +368,24 @@
         for m in range(1, 8):
             yb(m).start()
 
-    lax.fori_loop(8, LEAVES, nearby, 0, unroll=2)
+    for t in range(LEAVES):
+        pts[t] = gp[pl.ds(starts[t], LEAF), :].astype(BF16)
+
+    eye = (
+        lax.broadcasted_iota(jnp.int32, (LEAF, LEAF), 0) == lax.broadcasted_iota(jnp.int32, (LEAF, LEAF), 1)
+    ).astype(F32)
+    shift = (
+        lax.broadcasted_iota(jnp.int32, (R, R), 0) == lax.broadcasted_iota(jnp.int32, (R, R), 1) + 64
+    ).astype(F32).astype(BF16)
+
+    def nearby(t, carry):
+        left = pts[t]
+        right = dot(left, shift).astype(BF16)
+        kernel = (jnp.exp(dot(left, right, 1, 1)) + eye).astype(BF16)
+        near[t] = dot(kernel, rows[t])
+        return carry
+
+    lax.fori_loop(0, 4, nearby, 0, unroll=4)
 
     @pl.when(is0)
     def _():
@@ -407,6 +408,10 @@
         for m in range(1, 8):
             zs(m).start()
 
+    lax.fori_loop(4, LEAVES, nearby, 0, unroll=4)
+
+    @pl.when(is0)
+    def _():
         for m in range(1, 8):
             m5_from(m).wait_recv()
         mat_w[6] = xlev[:, 0].reshape(R, R).astype(BF16)
@@ -417,6 +422,8 @@
 
         for m in range(1, 8):
             zs(m).wait_recv()
+        u = zsend[0, 1]
+        for m in range(1, 8):
             u = u + zgot[m, 1]
         xsend[0] = u
         xsend[1] = mm(u, mat_w[6])
@@ -462,23 +469,13 @@
     across = jnp.where(is0, c.T, c).astype(BF16)
     field[30] = mmt(up_field[...], weight) + mm(core_coef[...], across)
 
-    def descend(i, carry):
-        j = 14 - i
+    for j in range(14, -1, -1):
         both = mmt(field[16 + j], transfer[j])
         field[2 * j] = both[:, :R] + term[2 * j]
         field[2 * j + 1] = both[:, R:] + term[2 * j + 1]
-        return carry
-
-    descend(0, 0)
-    lax.fori_loop(1, 3, descend, 0, unroll=2)
-    lax.fori_loop(3, 7, descend, 0, unroll=4)
-    lax.fori_loop(7, 15, descend, 0, unroll=4)
-
-    def finish(t, carry):
+
+    for t in range(LEAVES):
         total[t] = (near[t] + dot(basis[t], field[t].astype(BF16), 1, 1)).astype(BF16)
-        return carry
-
-    lax.fori_loop(0, LEAVES, finish, 0, unroll=4)
 
     @pl.when(is1)
     def _():
@@ -509,15 +506,25 @@
                 group(m).wait_send()
 
 
-def tree(rows, pts, basis, transfer, coupling, ctrans, ccoup):
+def tree(order, sizes, values, points, basis, transfer, coupling, ctrans, ccoup):
     dma = pltpu.SemaphoreType.DMA
     block = (R, R)
     return pl.pallas_call(
         tree_kernel,
         out_shape=jax.ShapeDtypeStruct((LEAVES, LEAF, R), BF16),
-        in_specs=[VMEM] * 7,
+        in_specs=[SMEM, SMEM, VMEM, VMEM, HBM, HBM, HBM, VMEM, VMEM],
         out_specs=VMEM,
         scratch_shapes=[
+            pltpu.VMEM((LEAVES, LEAF, R), BF16),
+            pltpu.VMEM((LEAVES - 1, 2 * R, R), BF16),
+            pltpu.VMEM((LEAVES - 1,) + block, BF16),
+            dma((3,)),
+            pltpu.VMEM((PTS, R), F32),
+            pltpu.VMEM((PTS, R), F32),
+            pltpu.VMEM((PTS + LEAF, R), F32),
+            pltpu.VMEM((PTS + LEAF, R), F32),
+            pltpu.VMEM((LEAVES, LEAF, R), BF16),
+            pltpu.VMEM((LEAVES, LEAF, R), BF16),
             pltpu.VMEM((31,) + block, F32),
             pltpu.VMEM((30,) + block, F32),
             pltpu.VMEM((31,) + block, F32),
@@ -543,7 +550,7 @@
             pltpu.VMEM((16, R), F32),
             pltpu.VMEM((8, 16, R), F32),
             dma((3,)), dma((3,)),
-            dma((8,)), dma((3,)),
+            dma((2, 8)), dma((2, 3)),
             dma((8,)), dma,
             dma((8,)), dma((8,)),
             dma((4,)), dma((4,)),
@@ -559,7 +566,7 @@
             collective_id=0, has_side_effects=True, vmem_limit_bytes=VMEM_LIMIT
         ),
         name="tree",
-    )(rows, pts, basis, transfer, coupling, ctrans, ccoup)
+    )(order, sizes, values, points, basis, transfer, coupling, ctrans, ccoup)
 
 
 def body(
@@ -573,9 +580,11 @@
     cross_transfer,
     cross_coupling,
 ):
-    rows, pts = gather(values, points, tree_order, leaf_sizes)
     transfer = local_transfer.reshape(LEAVES - 1, 2 * R, R)
-    total = tree(rows, pts, leaf_basis, transfer, local_coupling, cross_transfer, cross_coupling)
+    total = tree(
+        tree_order, leaf_sizes, values, points,
+        leaf_basis, transfer, local_coupling, cross_transfer, cross_coupling,
+    )
     return scatter(total, tree_order, leaf_sizes)
 
 

time: 70.8 us -> 61 us (0.86)
  Pallas kernels: 70.5 us -> 60.8 us
    pallas_call x1 -> x0, Pallas kernels: 6.99 us -> none  [gather(): pl.pallas_call(gather_kernel, out_shape=[jax.ShapeDtypeStruct((LEAVES, LE...]
    pallas_call x1, Pallas kernels: 58.3 us -> 55.6 us  [tree(): pl.pallas_call(tree_kernel, out_shape=jax.ShapeDtypeStruct((LEAVES, LEAF,...]
where the time goes in v2:
time: 61 us; the launch traced here: 60.8 us
  Pallas kernels  60.8 us (100%)
    pallas_call x1, Pallas kernels, tree(): pl.pallas_call(tree_kernel, out_shape=jax.ShapeDtypeStruct((LEAVES, LEAF,...  55.6 us
    pallas_call x1, Pallas kernels, scatter(): pl.pallas_call(scatter_kernel, out_shape=jax.ShapeDtypeStruct((PTS, R), B...  5.21 us

profile of v2, /device:TPU:1, one launch (start us, length us, event | category | flops | bytes accessed | tf_op | source)
XLA Modules:
  0.0 60.8 jit_solution(14762100023118541093)
XLA Ops:
  0.0 55.6 %tree.1.total = bf16[16,256,128]{2,1,0:T(8,128)(2,1)} custom-call(s32[1,3072]{1,0:T(1,128)} %order.3, s32[1,16]{1,0:T(1,128)} %sizes.3, bf16[3072,128]{1,0:T(8,128)(2,1)} %v_ref.1, f32[8,3072]{1,0:T(8,128)} %p_ref.1, bf16[16,256,128]{2,1,0:T(8,128)(2,1)} %basis_any.1, bf16[15,256,128]{2,1,0:T(8,128)(2,1)} %bitcast.1, bf16[15,128,128]{2,1,0:T(8,128)(2,1)} %coupling_any.1, ...), custom_call_target="tpu_custom_call" | custom-call | tf_op jit(solution)/shard_map/tree/pallas_call | solution.py:512
  55.6 5.2 %scatter_rows.1 = bf16[3072,128]{1,0:T(8,128)(2,1)} custom-call(s32[1,3072]{1,0:T(1,128)} %order.3, s32[1,16]{1,0:T(1,128)} %sizes.3, bf16[16,256,128]{2,1,0:T(8,128)(2,1)} %tree.1.total), custom_call_target="tpu_custom_call" | custom-call | tf_op jit(solution)/shard_map/scatter_rows/pallas_call | solution.py:63

commit v3 on v2

--- a/solution.py
+++ b/solution.py
@@ -19,7 +19,7 @@
 LEAF = 256
 LEAVES = 16
 R = 128
-UNROLL = 32
+UNROLL = 64
 
 
 def point_pieces(p):
@@ -108,11 +108,11 @@
 
 def tree_kernel(
     order, sizes, v_ref, p_ref, basis_any, transfer_any, coupling_any, ctrans, ccoup, total,
-    basis, transfer, coupling, s_local, tv, tp, gv, gp, rows, pts,
+    v_in, p_in, basis, transfer, coupling, s_local, tv, tp, gv, gp, rows, pts,
     coef, term, field, near, own, core_mats, core_coef, up_field,
-    path, piece, xpiece, zlev, xlev, mat_w, mat_c,
+    path, piece, wpiece, wlev, xpiece, xpath, xlev, mat_w, mat_c,
     prod, yslice, yblock, zsend, zgot, xsend, xgot, gdown, fdown,
-    s_core, r_core, s_dir, r_dir, s_m1, r_m1, s_m2, r_m2, s_m3, r_m3, s_m4, r_m4, s_m5, r_m5,
+    s_core, r_core, s_dir, r_dir, s_m1, r_m1, s_mw, r_mw, s_m4w, r_m4w, s_m2, r_m2, s_m3, r_m3, s_mx, r_mx, s_m5, r_m5,
     s_ys, r_ys, s_yb, r_yb, s_z, r_z, s_x, r_x, s_yd, r_yd,
 ):
     me = lax.axis_index("leaf")
@@ -139,7 +139,7 @@
     loads = [
         pltpu.make_async_copy(src, dst, s_local.at[i])
         for i, (src, dst) in enumerate(
-            [(basis_any, basis), (transfer_any, transfer), (coupling_any, coupling)]
+            [(v_ref, v_in), (p_ref, p_in), (basis_any, basis), (transfer_any, transfer), (coupling_any, coupling)]
         )
     ]
     for load in loads:
@@ -157,7 +157,8 @@
         for to in along_y[1:] + along_z[1:] + along_x[1:]:
             pl.semaphore_signal(barrier, inc=1, device_id=(to,), device_id_type=MESH)
 
-    tv[...] = v_ref[...].astype(F32)
+    loads[0].wait()
+    tv[...] = v_in[...].astype(F32)
     gv[PTS:, :] = jnp.zeros((LEAF, R), F32)
     gp[PTS:, :] = jnp.zeros((LEAF, R), F32)
 
@@ -186,31 +187,42 @@
         to = at(x, z, y - half + i)
         return copy(src, path.at[level, which], s_dir.at[which, i], r_dir.at[which, level], to)
 
-    def direct_all(level):
+    def direct_all(level, which):
         size = 2 << level
-        return [direct(level, i, which) for which in range(2) for i in range(size) if i != size // 2]
+        return [direct(level, i, which) for i in range(size) if i != size // 2]
 
     def m1(k):
         return copy(own.at[:, 16 * k : 16 * k + 16, :], piece.at[z], s_m1.at[k], r_m1, at(x, z, k))
 
+    def mw(m):
+        to = flip(z, m)
+        side = jnp.where(to < z, 0, 2)
+        return copy(piece.at[z, side], wpiece.at[z], s_mw.at[m], r_mw.at[m], along_z[m])
+
+    def mw_from(m):
+        return copy(piece.at[z, 0], wpiece.at[flip(z, m)], s_mw.at[m], r_mw.at[m], along_z[m])
+
+    def m4w(m):
+        return copy(wlev.at[y], wlev.at[y], s_m4w.at[m], r_m4w.at[m], along_y[m])
+
+    def m4w_from(m):
+        return copy(wlev.at[y], wlev.at[flip(y, m)], s_m4w.at[m], r_m4w.at[m], along_y[m])
+
     def m2(m):
-        return copy(piece.at[z], piece.at[z], s_m2.at[m], r_m2.at[m], along_z[m])
+        return copy(piece.at[z, 1], piece.at[z, 1], s_m2.at[m], r_m2.at[m], along_z[m])
 
     def m2_from(m):
-        there = piece.at[flip(z, m)]
+        there = piece.at[flip(z, m), 1]
         return copy(there, there, s_m2.at[m], r_m2.at[m], along_z[m])
 
     def m3(m):
         return copy(piece.at[0], xpiece.at[x], s_m3.at[m], r_m3.at[m], along_x[m])
 
+    def mx(m):
+        return copy(xpath, xpath, s_mx.at[m], r_mx, at(x, m, y))
+
     def m3_from(m):
         return copy(piece.at[0], xpiece.at[flip(x, m)], s_m3.at[m], r_m3.at[m], along_x[m])
-
-    def m4(m):
-        return copy(zlev.at[y], zlev.at[y], s_m4.at[m], r_m4.at[m], along_y[m])
-
-    def m4_from(m):
-        return copy(zlev.at[y], zlev.at[flip(y, m)], s_m4.at[m], r_m4.at[m], along_y[m])
 
     def m5(m):
         return copy(xlev.at[y], xlev.at[y], s_m5.at[m], r_m5.at[m], along_y[m])
@@ -255,10 +267,19 @@
 
             @pl.when(lax.rem(y, size) == size // 2)
             def _():
-                for c in direct_all(level):
+                for c in direct_all(level, 0):
                     c.start()
                 path[level, 0] = own[2]
                 path[level, 1] = own[1]
+
+    def wait_path(which):
+        for level in range(3):
+            size = 2 << level
+
+            @pl.when(lax.rem(y, size) != size // 2)
+            def _():
+                got = path.at[level, which]
+                copy(own.at[0], got, s_dir.at[0, 0], r_dir.at[which, level], mate).wait_recv()
 
     def permute(table, placed, first, last):
         def move(i, carry):
@@ -271,102 +292,97 @@
 
     permute(tv, gv, 0, PTS)
 
-    @pl.when(is0)
-    def _():
-        @pl.when(y > 0)
-        def _():
-            m1(1).wait_recv()
-
-        for m in range(1, 8):
-            m2(m).start()
-
     slot = lax.broadcasted_iota(jnp.int32, (LEAF, R), 0)
     starts = [0]
     for t in range(LEAVES):
         size = sizes[0, t]
         rows[t] = jnp.where(slot < size, gv[pl.ds(starts[t], LEAF), :], 0.0).astype(BF16)
         starts.append(starts[t] + size)
-    loads[0].wait()
+    loads[2].wait()
     for t in range(LEAVES):
         coef[t] = dot(rows[t], basis[t], 0, 0)
-    loads[1].wait()
+    loads[3].wait()
     for j in range(15):
         both = jnp.concatenate([coef[2 * j], coef[2 * j + 1]], axis=1)
         coef[16 + j] = mm(both, transfer[j])
     c_coef().start()
 
-    loads[2].wait()
+    @pl.when(is0)
+    def _():
+        @pl.when(y > 0)
+        def _():
+            m1(1).wait_recv()
+
+        for m in range(1, 8):
+            mw(m).start()
+        for m in range(1, 8):
+            m2(m).start()
+        wpiece[z] = piece[z, 2]
+
+        @pl.when(z == 0)
+        def _():
+            for m in range(1, 4):
+                m3(m).start()
+            xpiece[x] = piece[0]
+
+    loads[4].wait()
     for j in range(15):
         term[2 * j] = mmt(coef[2 * j + 1], coupling[j])
         term[2 * j + 1] = mm(coef[2 * j], coupling[j])
 
     @pl.when(is0)
     def _():
-        for which in range(2):
-            for level in range(3):
-                size = 2 << level
-
-                @pl.when(lax.rem(y, size) != size // 2)
-                def _():
-                    copy(
-                        own.at[0], path.at[level, which], s_dir.at[0, 0], r_dir.at[which, level], mate
-                    ).wait_recv()
-
-                if which == 0:
-                    mat_w[level] = path[level, 0].astype(BF16)
-            if which == 0:
-                c_mats().wait_recv()
-                c_coef().wait()
-                pair = jnp.concatenate([core_mats[0], core_mats[2]], axis=0).astype(BF16)
-                prod[0] = mm(jnp.concatenate([coef[30], core_coef[...]], axis=1), pair)
-                for level in range(3):
-                    prod[level + 1] = mm(prod[level], mat_w[level])
-                for m in range(1, 8):
-                    ys(m).start()
-                yslice[0] = prod[3, pl.ds(pl.multiple_of(16 * y, 16), 16), :]
+        wait_path(0)
         for level in range(3):
-            c = path[level, 1]
-            mat_c[level] = jnp.where(lax.rem(lax.div(y, 1 << level), 2) == 0, c.T, c).astype(BF16)
+            mat_w[level] = path[level, 0].astype(BF16)
+        c_mats().wait_recv()
+        c_coef().wait()
+        pair = jnp.concatenate([core_mats[0], core_mats[2]], axis=0).astype(BF16)
+        prod[0] = mm(jnp.concatenate([coef[30], core_coef[...]], axis=1), pair)
+        for level in range(3):
+            prod[level + 1] = mm(prod[level], mat_w[level])
+        for m in range(1, 8):
+            ys(m).start()
+        for lev in range(3):
+
+            @pl.when(lax.rem(y, 2 << lev) == 1 << lev)
+            def _():
+                for c in direct_all(lev, 1):
+                    c.start()
+
+        yslice[0] = prod[3, pl.ds(pl.multiple_of(16 * y, 16), 16), :]
 
     @pl.when(is1)
     def _():
         c_coef().wait()
 
+    loads[1].wait()
     for c in range(PTS // 128):
         span = slice(128 * c, 128 * (c + 1))
-        tp[span, :] = point_pieces(p_ref[:, span]).T
-    permute(tp, gp, 0, PTS // 4)
-
-    @pl.when(is0)
-    def _():
-        for m in range(1, 8):
-            m2_from(m).wait_recv()
-        for m in range(1, 4):
-            m3(m).start()
-        xpiece[x] = piece[0]
-        for i in range(3):
-            half = 1 << i
-            owner = lax.div(z, 2 * half) * 2 * half + half
-            side = lax.rem(lax.div(z, half), 2)
-            zlev[y, 2 * i] = piece[owner, 2 * side]
-            zlev[y, 2 * i + 1] = piece[owner, 1]
-        for m in range(1, 8):
-            m4(m).start()
-
-    permute(tp, gp, PTS // 4, PTS)
-
-    @pl.when(is0)
+        tp[span, :] = point_pieces(p_in[:, span]).T
+    @pl.when(jnp.logical_and(is0, z == 0))
     def _():
         for m in range(1, 4):
             m3_from(m).wait_recv()
         owner = lax.div(x, 2) * 2 + 1
-        xlev[y, 0] = xpiece[owner, 2 * lax.rem(x, 2)]
-        xlev[y, 1] = xpiece[owner, 1]
-        xlev[y, 2] = xpiece[2, 1]
-        for m in range(1, 8):
-            m5(m).start()
-        for m in range(1, 8):
-            yb(m).start()
+        xpath[0] = xpiece[owner, 1]
+        xpath[1] = xpiece[2, 1]
+        xpath[2] = xpiece[owner, 2 * lax.rem(x, 2)]
+        for m in range(1, 8):
+            mx(m).start()
+
+    permute(tp, gp, 0, PTS // 2)
+
+    @pl.when(is0)
+    def _():
+        for m in range(1, 8):
+            mw_from(m).wait_recv()
+        for i in range(3):
+            wlev[y, i] = wpiece[lax.div(z, 2 << i) * (2 << i) + (1 << i)]
+        for m in range(1, 8):
+            m4w(m).start()
+
+    permute(tp, gp, PTS // 2, PTS)
 
     for t in range(LEAVES):
         pts[t] = gp[pl.ds(starts[t], LEAF), :].astype(BF16)
@@ -390,11 +406,26 @@
     @pl.when(is0)
     def _():
         for m in range(1, 8):
-            m4_from(m).wait_recv()
+            m2_from(m).wait_recv()
+
+        @pl.when(z > 0)
+        def _():
+            mx(1).wait_recv()
+
         for i in range(3):
-            mat_w[3 + i] = zlev[:, 2 * i].reshape(R, R).astype(BF16)
-            c = zlev[:, 2 * i + 1].reshape(R, R)
-            mat_c[3 + i] = jnp.where(lax.rem(lax.div(z, 1 << i), 2) == 0, c.T, c).astype(BF16)
+            xlev[y, i] = piece[lax.div(z, 2 << i) * (2 << i) + (1 << i), 1]
+        xlev[y, 3:6] = xpath[...]
+        for m in range(1, 8):
+            m5(m).start()
+        for m in range(1, 8):
+            yb(m).start()
+
+    @pl.when(is0)
+    def _():
+        for m in range(1, 8):
+            m4w_from(m).wait_recv()
+        for i in range(3):
+            mat_w[3 + i] = wlev[:, i].reshape(R, R).astype(BF16)
         for m in range(1, 8):
             ys(m).wait_recv()
         u = yslice[0]
@@ -414,11 +445,7 @@
     def _():
         for m in range(1, 8):
             m5_from(m).wait_recv()
-        mat_w[6] = xlev[:, 0].reshape(R, R).astype(BF16)
-        c = xlev[:, 1].reshape(R, R)
-        mat_c[6] = jnp.where(lax.rem(x, 2) == 0, c.T, c).astype(BF16)
-        c = xlev[:, 2].reshape(R, R)
-        mat_c[7] = jnp.where(lax.div(x, 2) == 0, c.T, c).astype(BF16)
+        mat_w[6] = xlev[:, 5].reshape(R, R).astype(BF16)
 
         for m in range(1, 8):
             zs(m).wait_recv()
@@ -429,6 +456,10 @@
         xsend[1] = mm(u, mat_w[6])
         for m in range(1, 4):
             xs(m).start()
+        sides = [lax.rem(lax.div(z, 1 << i), 2) for i in range(3)] + [lax.rem(x, 2), lax.div(x, 2)]
+        for i in range(5):
+            c = xlev[:, i].reshape(R, R)
+            mat_c[3 + i] = jnp.where(sides[i] == 0, c.T, c).astype(BF16)
         side_z = [
             mm(zgot[1, 0], mat_c[3]),
             mm(zgot[2, 0] + zgot[3, 0], mat_c[4]),
@@ -445,6 +476,10 @@
             yd(m).start()
         fdown[y] = g
 
+        wait_path(1)
+        for level in range(3):
+            c = path[level, 1]
+            mat_c[level] = jnp.where(lax.rem(lax.div(y, 1 << level), 2) == 0, c.T, c).astype(BF16)
         for m in range(1, 8):
             yb(m).wait_recv()
         side_y = [
@@ -495,15 +530,21 @@
 
             @pl.when(lax.rem(y, size) == size // 2)
             def _():
-                for c in direct_all(level):
+                for c in direct_all(level, 0) + direct_all(level, 1):
                     c.wait_send()
 
         for m in range(1, 8):
-            for group in (m2, m4, m5, ys, yb, zs, yd):
+            for group in (mw, m4w, m2, m5, ys, yb, zs, yd):
                 group(m).wait_send()
         for m in range(1, 4):
-            for group in (m3, xs):
-                group(m).wait_send()
+            xs(m).wait_send()
+
+        @pl.when(z == 0)
+        def _():
+            for m in range(1, 4):
+                m3(m).wait_send()
+            for m in range(1, 8):
+                mx(m).wait_send()
 
 
 def tree(order, sizes, values, points, basis, transfer, coupling, ctrans, ccoup):
@@ -512,13 +553,15 @@
     return pl.pallas_call(
         tree_kernel,
         out_shape=jax.ShapeDtypeStruct((LEAVES, LEAF, R), BF16),
-        in_specs=[SMEM, SMEM, VMEM, VMEM, HBM, HBM, HBM, VMEM, VMEM],
+        in_specs=[SMEM, SMEM, HBM, HBM, HBM, HBM, HBM, VMEM, VMEM],
         out_specs=VMEM,
         scratch_shapes=[
+            pltpu.VMEM((PTS, R), BF16),
+            pltpu.VMEM((8, PTS), F32),
             pltpu.VMEM((LEAVES, LEAF, R), BF16),
             pltpu.VMEM((LEAVES - 1, 2 * R, R), BF16),
             pltpu.VMEM((LEAVES - 1,) + block, BF16),
-            dma((3,)),
+            dma((5,)),
             pltpu.VMEM((PTS, R), F32),
             pltpu.VMEM((PTS, R), F32),
             pltpu.VMEM((PTS + LEAF, R), F32),
@@ -535,9 +578,11 @@
             pltpu.VMEM(block, F32),
             pltpu.VMEM((3, 2) + block, F32),
             pltpu.VMEM((8, 3, 16, R), F32),
+            pltpu.VMEM((8, 16, R), F32),
+            pltpu.VMEM((8, 3, 16, R), F32),
             pltpu.VMEM((4, 3, 16, R), F32),
+            pltpu.VMEM((3, 16, R), F32),
             pltpu.VMEM((8, 6, 16, R), F32),
-            pltpu.VMEM((8, 3, 16, R), F32),
             pltpu.VMEM((7,) + block, BF16),
             pltpu.VMEM((8,) + block, BF16),
             pltpu.VMEM((4,) + block, F32),
@@ -553,8 +598,10 @@
             dma((2, 8)), dma((2, 3)),
             dma((8,)), dma,
             dma((8,)), dma((8,)),
+            dma((8,)), dma((8,)),
+            dma((8,)), dma((8,)),
             dma((4,)), dma((4,)),
-            dma((8,)), dma((8,)),
+            dma((8,)), dma,
             dma((8,)), dma((8,)),
             dma((8,)), dma((8,)),
             dma((8,)), dma((8,)),

time: 61 us -> 58.2 us (0.954)
  Pallas kernels: 60.8 us -> 57.9 us
    pallas_call x1, Pallas kernels: 55.6 us -> 52.9 us  [tree(): pl.pallas_call(tree_kernel, out_shape=jax.ShapeDtypeStruct((LEAVES, LEAF,...]
where the time goes in v3:
time: 58.2 us; the launch traced here: 57.9 us
  Pallas kernels  57.9 us (99%)
    pallas_call x1, Pallas kernels, tree(): pl.pallas_call(tree_kernel, out_shape=jax.ShapeDtypeStruct((LEAVES, LEAF,...  52.9 us
    pallas_call x1, Pallas kernels, scatter(): pl.pallas_call(scatter_kernel, out_shape=jax.ShapeDtypeStruct((PTS, R), B...  4.98 us

profile of v3, /device:TPU:1, one launch (start us, length us, event | category | flops | bytes accessed | tf_op | source)
XLA Modules:
  0.0 57.9 jit_solution(5142534205231798182)
XLA Ops:
  0.0 52.9 %tree.1.total = bf16[16,256,128]{2,1,0:T(8,128)(2,1)} custom-call(s32[1,3072]{1,0:T(1,128)} %order.3, s32[1,16]{1,0:T(1,128)} %sizes.3, bf16[3072,128]{1,0:T(8,128)(2,1)} %v_ref.1, f32[8,3072]{1,0:T(8,128)} %p_ref.1, bf16[16,256,128]{2,1,0:T(8,128)(2,1)} %basis_any.1, bf16[15,256,128]{2,1,0:T(8,128)(2,1)} %bitcast.1, bf16[15,128,128]{2,1,0:T(8,128)(2,1)} %coupling_any.1, ...), custom_call_target="tpu_custom_call" | custom-call | tf_op jit(solution)/shard_map/tree/pallas_call | solution.py:553
  52.9 5.0 %scatter_rows.1 = bf16[3072,128]{1,0:T(8,128)(2,1)} custom-call(s32[1,3072]{1,0:T(1,128)} %order.3, s32[1,16]{1,0:T(1,128)} %sizes.3, bf16[16,256,128]{2,1,0:T(8,128)(2,1)} %tree.1.total), custom_call_target="tpu_custom_call" | custom-call | tf_op jit(solution)/shard_map/scatter_rows/pallas_call | solution.py:63

commit v4 on v3

--- a/solution.py
+++ b/solution.py
@@ -19,7 +19,8 @@
 LEAF = 256
 LEAVES = 16
 R = 128
-UNROLL = 64
+UNROLL = 128
+FAR_FIRST = (4, 5, 3, 7, 6, 2, 1)
 
 
 def point_pieces(p):
@@ -69,7 +70,7 @@
             pltpu.VMEM((PTS + LEAF, R), F32),
             pltpu.VMEM((PTS, R), F32),
         ],
-        compiler_params=pltpu.CompilerParams(vmem_limit_bytes=VMEM_LIMIT),
+        compiler_params=pltpu.CompilerParams(vmem_limit_bytes=56 * 2**20),
         name="scatter_rows",
     )(order, sizes, total)
 
@@ -91,6 +92,26 @@
 def mmt(x, w):
     y = dot(split(x), w, 1, 1)
     return y[: x.shape[0]] + y[x.shape[0] :]
+
+
+def mmt3(x, w):
+    h = w.astype(BF16)
+    return mmt(x, h) + dot(x.astype(BF16), (w - h.astype(F32)).astype(BF16), 1, 1)
+
+
+def mm3(x, w):
+    h = w.astype(BF16)
+    return mm(x, h) + dot(x.astype(BF16), (w - h.astype(F32)).astype(BF16))
+
+
+def exact_mmt(x, w):
+    h = w.astype(BF16)
+    return dot(x, h, 1, 1) + dot(x, (w - h.astype(F32)).astype(BF16), 1, 1)
+
+
+def exact_mm(x, w):
+    h = w.astype(BF16)
+    return dot(x, h) + dot(x, (w - h.astype(F32)).astype(BF16))
 
 
 def flip(v, m):
@@ -111,7 +132,7 @@
     v_in, p_in, basis, transfer, coupling, s_local, tv, tp, gv, gp, rows, pts,
     coef, term, field, near, own, core_mats, core_coef, up_field,
     path, piece, wpiece, wlev, xpiece, xpath, xlev, mat_w, mat_c,
-    prod, yslice, yblock, zsend, zgot, xsend, xgot, gdown, fdown,
+    far, prod, yslice, yblock, zsend, zgot, xsend, xgot, gdown, fdown,
     s_core, r_core, s_dir, r_dir, s_m1, r_m1, s_mw, r_mw, s_m4w, r_m4w, s_m2, r_m2, s_m3, r_m3, s_mx, r_mx, s_m5, r_m5,
     s_ys, r_ys, s_yb, r_yb, s_z, r_z, s_x, r_x, s_yd, r_yd,
 ):
@@ -136,6 +157,14 @@
             src_ref=src, dst_ref=dst, send_sem=send, recv_sem=recv, device_id=(to,), device_id_type=MESH
         )
 
+    barrier = pltpu.get_barrier_semaphore()
+    pl.semaphore_signal(barrier, inc=1, device_id=(mate,), device_id_type=MESH)
+
+    @pl.when(is0)
+    def _():
+        for to in along_y[1:] + along_z[1:] + along_x[1:]:
+            pl.semaphore_signal(barrier, inc=1, device_id=(to,), device_id_type=MESH)
+
     loads = [
         pltpu.make_async_copy(src, dst, s_local.at[i])
         for i, (src, dst) in enumerate(
@@ -149,14 +178,6 @@
     own[1] = ccoup[0].astype(F32)
     own[2] = ctrans[0, 1].astype(F32)
 
-    barrier = pltpu.get_barrier_semaphore()
-    pl.semaphore_signal(barrier, inc=1, device_id=(mate,), device_id_type=MESH)
-
-    @pl.when(is0)
-    def _():
-        for to in along_y[1:] + along_z[1:] + along_x[1:]:
-            pl.semaphore_signal(barrier, inc=1, device_id=(to,), device_id_type=MESH)
-
     loads[0].wait()
     tv[...] = v_in[...].astype(F32)
     gv[PTS:, :] = jnp.zeros((LEAF, R), F32)
@@ -177,7 +198,7 @@
         return copy(coef.at[30], core_coef, s_core.at[1], r_core.at[1], mate)
 
     def c_field():
-        return copy(up_field, up_field, s_core.at[2], r_core.at[2], mate)
+        return copy(up_field, field.at[30], s_core.at[2], r_core.at[2], mate)
 
 
     def direct(level, i, which):
@@ -252,13 +273,12 @@
     @pl.when(is1)
     def _():
         c_mats().start()
-        core_mats[...] = own[...]
 
     @pl.when(is0)
     def _():
         @pl.when(y == 0)
         def _():
-            for k in range(1, 8):
+            for k in (4, 3, 5, 2, 6, 1, 7):
                 m1(k).start()
             piece[z] = own[:, 0:16, :]
 
@@ -313,15 +333,15 @@
         def _():
             m1(1).wait_recv()
 
-        for m in range(1, 8):
+        for m in FAR_FIRST:
             mw(m).start()
-        for m in range(1, 8):
+        for m in FAR_FIRST:
             m2(m).start()
         wpiece[z] = piece[z, 2]
 
         @pl.when(z == 0)
         def _():
-            for m in range(1, 4):
+            for m in (2, 3, 1):
                 m3(m).start()
             xpiece[x] = piece[0]
 
@@ -341,7 +361,7 @@
         prod[0] = mm(jnp.concatenate([coef[30], core_coef[...]], axis=1), pair)
         for level in range(3):
             prod[level + 1] = mm(prod[level], mat_w[level])
-        for m in range(1, 8):
+        for m in FAR_FIRST:
             ys(m).start()
         for lev in range(3):
 
@@ -368,7 +388,7 @@
         xpath[0] = xpiece[owner, 1]
         xpath[1] = xpiece[2, 1]
         xpath[2] = xpiece[owner, 2 * lax.rem(x, 2)]
-        for m in range(1, 8):
+        for m in FAR_FIRST:
             mx(m).start()
 
     permute(tp, gp, 0, PTS // 2)
@@ -379,7 +399,7 @@
             mw_from(m).wait_recv()
         for i in range(3):
             wlev[y, i] = wpiece[lax.div(z, 2 << i) * (2 << i) + (1 << i)]
-        for m in range(1, 8):
+        for m in FAR_FIRST:
             m4w(m).start()
 
     permute(tp, gp, PTS // 2, PTS)
@@ -415,10 +435,8 @@
         for i in range(3):
             xlev[y, i] = piece[lax.div(z, 2 << i) * (2 << i) + (1 << i), 1]
         xlev[y, 3:6] = xpath[...]
-        for m in range(1, 8):
+        for m in FAR_FIRST:
             m5(m).start()
-        for m in range(1, 8):
-            yb(m).start()
 
     @pl.when(is0)
     def _():
@@ -436,8 +454,10 @@
             u = mm(u, mat_w[3 + i])
         for i in range(3):
             zsend[i, 1] = u
-        for m in range(1, 8):
+        for m in FAR_FIRST:
             zs(m).start()
+        for m in FAR_FIRST:
+            yb(m).start()
 
     lax.fori_loop(4, LEAVES, nearby, 0, unroll=4)
 
@@ -454,7 +474,7 @@
             u = u + zgot[m, 1]
         xsend[0] = u
         xsend[1] = mm(u, mat_w[6])
-        for m in range(1, 4):
+        for m in (2, 3, 1):
             xs(m).start()
         sides = [lax.rem(lax.div(z, 1 << i), 2) for i in range(3)] + [lax.rem(x, 2), lax.div(x, 2)]
         for i in range(5):
@@ -465,14 +485,16 @@
             mm(zgot[2, 0] + zgot[3, 0], mat_c[4]),
             mm((zgot[4, 0] + zgot[5, 0]) + (zgot[6, 0] + zgot[7, 0]), mat_c[5]),
         ]
+        z_path = mm(dot(mat_w[3], mat_w[4]), mat_w[5])
+        x_path = mm(z_path, mat_w[6])
+        far[0:R] = exact_mmt(mat_c[7], x_path)
+        far[R:] = exact_mmt(mat_c[6], z_path)
+        before = mmt(mmt(side_z[2], mat_w[4]) + side_z[1], mat_w[3]) + side_z[0]
         for m in range(1, 4):
             xs(m).wait_recv()
-        g = mm(xgot[2] + xgot[3], mat_c[7])
-        g = mmt(g, mat_w[6]) + mm(xgot[1], mat_c[6])
-        for i in (2, 1, 0):
-            g = mmt(g, mat_w[3 + i]) + side_z[i]
+        g = mm3(jnp.concatenate([xgot[2] + xgot[3], xgot[1]], axis=1), far[...]) + before
         gdown[...] = g
-        for m in range(1, 8):
+        for m in FAR_FIRST:
             yd(m).start()
         fdown[y] = g
 
@@ -487,22 +509,23 @@
             mm(yblock[2] + yblock[3], mat_c[1]),
             mm((yblock[4] + yblock[5]) + (yblock[6] + yblock[7]), mat_c[2]),
         ]
+        pair = jnp.concatenate([core_mats[0], core_mats[2]], axis=0).astype(BF16)
+        between = core_mats[1].astype(BF16)
+        y_path = mm(dot(mat_w[0], mat_w[1]), mat_w[2])
+        far[...] = exact_mm(pair, y_path)
+        before = mmt(mmt(mmt(side_y[2], mat_w[1]) + side_y[1], mat_w[0]) + side_y[0], pair)
+        first = before[:, :R] + mmt(core_coef[...], between)
+        second = before[:, R:] + mm(coef[30], between)
         for m in range(1, 8):
             yd_from(m).wait_recv()
-        f = fdown[...].reshape(R, R)
-        for level in (2, 1, 0):
-            f = mmt(f, mat_w[level]) + side_y[level]
-        up_field[...] = f
+        both = mmt3(fdown[...].reshape(R, R), far[...])
+        up_field[...] = both[:, R:] + second
+        field[30] = both[:, :R] + first
         c_field().start()
 
     @pl.when(is1)
     def _():
         c_field().wait_recv()
-
-    weight = jnp.where(is0, core_mats[0], core_mats[2]).astype(BF16)
-    c = core_mats[1]
-    across = jnp.where(is0, c.T, c).astype(BF16)
-    field[30] = mmt(up_field[...], weight) + mm(core_coef[...], across)
 
     for j in range(14, -1, -1):
         both = mmt(field[16 + j], transfer[j])
@@ -585,6 +608,7 @@
             pltpu.VMEM((8, 6, 16, R), F32),
             pltpu.VMEM((7,) + block, BF16),
             pltpu.VMEM((8,) + block, BF16),
+            pltpu.VMEM((2 * R, R), F32),
             pltpu.VMEM((4,) + block, F32),
             pltpu.VMEM((8, 16, R), F32),
             pltpu.VMEM((8,) + block, F32),

time: 58.2 us -> 55.5 us (0.954)
  Pallas kernels: 57.9 us -> 55.2 us
    pallas_call x1, Pallas kernels: 52.9 us -> 50.3 us  [tree(): pl.pallas_call(tree_kernel, out_shape=jax.ShapeDtypeStruct((LEAVES, LEAF,...]
where the time goes in v4:
time: 55.5 us; the launch traced here: 55.2 us
  Pallas kernels  55.2 us (99%)
    pallas_call x1, Pallas kernels, tree(): pl.pallas_call(tree_kernel, out_shape=jax.ShapeDtypeStruct((LEAVES, LEAF,...  50.3 us
    pallas_call x1, Pallas kernels, scatter(): pl.pallas_call(scatter_kernel, out_shape=jax.ShapeDtypeStruct((PTS, R), B...  4.87 us

profile of v4, /device:TPU:1, one launch (start us, length us, event | category | flops | bytes accessed | tf_op | source)
XLA Modules:
  0.0 55.2 jit_solution(17321051164914522566)
XLA Ops:
  0.0 50.3 %tree.1.total = bf16[16,256,128]{2,1,0:T(8,128)(2,1)} custom-call(s32[1,3072]{1,0:T(1,128)} %order.3, s32[1,16]{1,0:T(1,128)} %sizes.3, bf16[3072,128]{1,0:T(8,128)(2,1)} %v_ref.1, f32[8,3072]{1,0:T(8,128)} %p_ref.1, bf16[16,256,128]{2,1,0:T(8,128)(2,1)} %basis_any.1, bf16[15,256,128]{2,1,0:T(8,128)(2,1)} %bitcast.1, bf16[15,128,128]{2,1,0:T(8,128)(2,1)} %coupling_any.1, ...), custom_call_target="tpu_custom_call" | custom-call | tf_op jit(solution)/shard_map/tree/pallas_call | solution.py:576
  50.3 4.9 %scatter_rows.1 = bf16[3072,128]{1,0:T(8,128)(2,1)} custom-call(s32[1,3072]{1,0:T(1,128)} %order.3, s32[1,16]{1,0:T(1,128)} %sizes.3, bf16[16,256,128]{2,1,0:T(8,128)(2,1)} %tree.1.total), custom_call_target="tpu_custom_call" | custom-call | tf_op jit(solution)/shard_map/scatter_rows/pallas_call | solution.py:64

commit v5 on v4

--- a/solution.py
+++ b/solution.py
@@ -131,9 +131,9 @@
     order, sizes, v_ref, p_ref, basis_any, transfer_any, coupling_any, ctrans, ccoup, total,
     v_in, p_in, basis, transfer, coupling, s_local, tv, tp, gv, gp, rows, pts,
     coef, term, field, near, own, core_mats, core_coef, up_field,
-    path, piece, wpiece, wlev, xpiece, xpath, xlev, mat_w, mat_c,
+    path, piece, wpiece, wlev, xpiece, xpath, w8lev, xlev, mat_w, mat_c,
     far, prod, yslice, yblock, zsend, zgot, xsend, xgot, gdown, fdown,
-    s_core, r_core, s_dir, r_dir, s_m1, r_m1, s_mw, r_mw, s_m4w, r_m4w, s_m2, r_m2, s_m3, r_m3, s_mx, r_mx, s_m5, r_m5,
+    s_core, r_core, s_dir, r_dir, s_m1, r_m1, s_mw, r_mw, s_m4w, r_m4w, s_m2, r_m2, s_m3, r_m3, s_mx, r_mx, s_m5, r_m5, s_m6, r_m6,
     s_ys, r_ys, s_yb, r_yb, s_z, r_z, s_x, r_x, s_yd, r_yd,
 ):
     me = lax.axis_index("leaf")
@@ -162,7 +162,8 @@
 
     @pl.when(is0)
     def _():
-        for to in along_y[1:] + along_z[1:] + along_x[1:]:
+        partners = [line[m] for m in FAR_FIRST for line in (along_y, along_z)]
+        for to in partners + along_x[1:]:
             pl.semaphore_signal(barrier, inc=1, device_id=(to,), device_id_type=MESH)
 
     loads = [
@@ -175,8 +176,8 @@
         load.start()
 
     own[0] = ctrans[0, 0].astype(F32)
-    own[1] = ccoup[0].astype(F32)
-    own[2] = ctrans[0, 1].astype(F32)
+    own[1] = ctrans[0, 1].astype(F32)
+    own[2] = ccoup[0].astype(F32)
 
     loads[0].wait()
     tv[...] = v_in[...].astype(F32)
@@ -204,7 +205,7 @@
     def direct(level, i, which):
         size = 2 << level
         half = size // 2
-        src = own.at[1] if which else own.at[0 if i < half else 2]
+        src = own.at[2] if which else own.at[0 if i < half else 1]
         to = at(x, z, y - half + i)
         return copy(src, path.at[level, which], s_dir.at[which, i], r_dir.at[which, level], to)
 
@@ -212,12 +213,15 @@
         size = 2 << level
         return [direct(level, i, which) for i in range(size) if i != size // 2]
 
-    def m1(k):
-        return copy(own.at[:, 16 * k : 16 * k + 16, :], piece.at[z], s_m1.at[k], r_m1, at(x, z, k))
+    def m1(k, part):
+        span, which = pl.ds(16 * k, 16), pl.ds(2 * part, 2 - part)
+        return copy(
+            own.at[which, span, :], piece.at[z, which], s_m1.at[part, k], r_m1.at[part], at(x, z, k)
+        )
 
     def mw(m):
         to = flip(z, m)
-        side = jnp.where(to < z, 0, 2)
+        side = jnp.where(to < z, 0, 1)
         return copy(piece.at[z, side], wpiece.at[z], s_mw.at[m], r_mw.at[m], along_z[m])
 
     def mw_from(m):
@@ -230,10 +234,10 @@
         return copy(wlev.at[y], wlev.at[flip(y, m)], s_m4w.at[m], r_m4w.at[m], along_y[m])
 
     def m2(m):
-        return copy(piece.at[z, 1], piece.at[z, 1], s_m2.at[m], r_m2.at[m], along_z[m])
+        return copy(piece.at[z, 2], piece.at[z, 2], s_m2.at[m], r_m2.at[m], along_z[m])
 
     def m2_from(m):
-        there = piece.at[flip(z, m), 1]
+        there = piece.at[flip(z, m), 2]
         return copy(there, there, s_m2.at[m], r_m2.at[m], along_z[m])
 
     def m3(m):
@@ -250,6 +254,12 @@
 
     def m5_from(m):
         return copy(xlev.at[y], xlev.at[flip(y, m)], s_m5.at[m], r_m5.at[m], along_y[m])
+
+    def m6(m):
+        return copy(w8lev.at[y], w8lev.at[y], s_m6.at[m], r_m6.at[m], along_y[m])
+
+    def m6_from(m):
+        return copy(w8lev.at[y], w8lev.at[flip(y, m)], s_m6.at[m], r_m6.at[m], along_y[m])
 
     def ys(m):
         part = prod.at[3, pl.ds(pl.multiple_of(16 * flip(y, m), 16), 16), :]
@@ -279,18 +289,20 @@
         @pl.when(y == 0)
         def _():
             for k in (4, 3, 5, 2, 6, 1, 7):
-                m1(k).start()
+                m1(k, 0).start()
+            for k in (4, 3, 5, 2, 6, 1, 7):
+                m1(k, 1).start()
             piece[z] = own[:, 0:16, :]
 
-        for level in range(3):
+        for level in (2,):
             size = 2 << level
 
             @pl.when(lax.rem(y, size) == size // 2)
             def _():
                 for c in direct_all(level, 0):
                     c.start()
-                path[level, 0] = own[2]
-                path[level, 1] = own[1]
+                path[level, 0] = own[1]
+                path[level, 1] = own[2]
 
     def wait_path(which):
         for level in range(3):
@@ -311,6 +323,19 @@
         lax.fori_loop(first // UNROLL, last // UNROLL, move, 0)
 
     permute(tv, gv, 0, PTS)
+
+    @pl.when(is0)
+    def _():
+        for level in (1, 0):
+            size = 2 << level
+
+            @pl.when(lax.rem(y, size) == size // 2)
+            def _():
+                for c in direct_all(level, 0):
+                    c.start()
+                path[level, 0] = own[1]
+                path[level, 1] = own[2]
+
 
     slot = lax.broadcasted_iota(jnp.int32, (LEAF, R), 0)
     starts = [0]
@@ -331,13 +356,15 @@
     def _():
         @pl.when(y > 0)
         def _():
-            m1(1).wait_recv()
+            m1(1, 0).wait_recv()
 
         for m in FAR_FIRST:
             mw(m).start()
-        for m in FAR_FIRST:
-            m2(m).start()
-        wpiece[z] = piece[z, 2]
+        wpiece[z] = piece[z, 1]
+
+        @pl.when(y > 0)
+        def _():
+            m1(1, 1).wait_recv()
 
         @pl.when(z == 0)
         def _():
@@ -345,6 +372,9 @@
                 m3(m).start()
             xpiece[x] = piece[0]
 
+        for m in FAR_FIRST:
+            m2(m).start()
+
     loads[4].wait()
     for j in range(15):
         term[2 * j] = mmt(coef[2 * j + 1], coupling[j])
@@ -357,7 +387,7 @@
             mat_w[level] = path[level, 0].astype(BF16)
         c_mats().wait_recv()
         c_coef().wait()
-        pair = jnp.concatenate([core_mats[0], core_mats[2]], axis=0).astype(BF16)
+        pair = jnp.concatenate([core_mats[0], core_mats[1]], axis=0).astype(BF16)
         prod[0] = mm(jnp.concatenate([coef[30], core_coef[...]], axis=1), pair)
         for level in range(3):
             prod[level + 1] = mm(prod[level], mat_w[level])
@@ -385,13 +415,11 @@
         for m in range(1, 4):
             m3_from(m).wait_recv()
         owner = lax.div(x, 2) * 2 + 1
-        xpath[0] = xpiece[owner, 1]
-        xpath[1] = xpiece[2, 1]
-        xpath[2] = xpiece[owner, 2 * lax.rem(x, 2)]
+        xpath[0] = xpiece[owner, 2]
+        xpath[1] = xpiece[2, 2]
+        xpath[2] = xpiece[owner, lax.rem(x, 2)]
         for m in FAR_FIRST:
             mx(m).start()
-
-    permute(tp, gp, 0, PTS // 2)
 
     @pl.when(is0)
     def _():
@@ -401,6 +429,8 @@
             wlev[y, i] = wpiece[lax.div(z, 2 << i) * (2 << i) + (1 << i)]
         for m in FAR_FIRST:
             m4w(m).start()
+
+    permute(tp, gp, 0, PTS // 2)
 
     permute(tp, gp, PTS // 2, PTS)
 
@@ -425,16 +455,18 @@
 
     @pl.when(is0)
     def _():
-        for m in range(1, 8):
-            m2_from(m).wait_recv()
-
         @pl.when(z > 0)
         def _():
             mx(1).wait_recv()
 
+        w8lev[y] = xpath[2]
+        for m in FAR_FIRST:
+            m6(m).start()
+        for m in range(1, 8):
+            m2_from(m).wait_recv()
         for i in range(3):
-            xlev[y, i] = piece[lax.div(z, 2 << i) * (2 << i) + (1 << i), 1]
-        xlev[y, 3:6] = xpath[...]
+            xlev[y, i] = piece[lax.div(z, 2 << i) * (2 << i) + (1 << i), 2]
+        xlev[y, 3:5] = xpath[0:2]
         for m in FAR_FIRST:
             m5(m).start()
 
@@ -459,13 +491,13 @@
         for m in FAR_FIRST:
             yb(m).start()
 
-    lax.fori_loop(4, LEAVES, nearby, 0, unroll=4)
-
-    @pl.when(is0)
-    def _():
-        for m in range(1, 8):
-            m5_from(m).wait_recv()
-        mat_w[6] = xlev[:, 5].reshape(R, R).astype(BF16)
+    lax.fori_loop(4, 12, nearby, 0, unroll=8)
+
+    @pl.when(is0)
+    def _():
+        for m in range(1, 8):
+            m6_from(m).wait_recv()
+        mat_w[6] = w8lev[...].reshape(R, R).astype(BF16)
 
         for m in range(1, 8):
             zs(m).wait_recv()
@@ -476,6 +508,13 @@
         xsend[1] = mm(u, mat_w[6])
         for m in (2, 3, 1):
             xs(m).start()
+
+    lax.fori_loop(12, LEAVES, nearby, 0, unroll=4)
+
+    @pl.when(is0)
+    def _():
+        for m in range(1, 8):
+            m5_from(m).wait_recv()
         sides = [lax.rem(lax.div(z, 1 << i), 2) for i in range(3)] + [lax.rem(x, 2), lax.div(x, 2)]
         for i in range(5):
             c = xlev[:, i].reshape(R, R)
@@ -509,8 +548,8 @@
             mm(yblock[2] + yblock[3], mat_c[1]),
             mm((yblock[4] + yblock[5]) + (yblock[6] + yblock[7]), mat_c[2]),
         ]
-        pair = jnp.concatenate([core_mats[0], core_mats[2]], axis=0).astype(BF16)
-        between = core_mats[1].astype(BF16)
+        pair = jnp.concatenate([core_mats[0], core_mats[1]], axis=0).astype(BF16)
+        between = core_mats[2].astype(BF16)
         y_path = mm(dot(mat_w[0], mat_w[1]), mat_w[2])
         far[...] = exact_mm(pair, y_path)
         before = mmt(mmt(mmt(side_y[2], mat_w[1]) + side_y[1], mat_w[0]) + side_y[0], pair)
@@ -546,7 +585,8 @@
         @pl.when(y == 0)
         def _():
             for k in range(1, 8):
-                m1(k).wait_send()
+                m1(k, 0).wait_send()
+                m1(k, 1).wait_send()
 
         for level in range(3):
             size = 2 << level
@@ -557,7 +597,7 @@
                     c.wait_send()
 
         for m in range(1, 8):
-            for group in (mw, m4w, m2, m5, ys, yb, zs, yd):
+            for group in (mw, m4w, m2, m5, m6, ys, yb, zs, yd):
                 group(m).wait_send()
         for m in range(1, 4):
             xs(m).wait_send()
@@ -605,7 +645,8 @@
             pltpu.VMEM((8, 3, 16, R), F32),
             pltpu.VMEM((4, 3, 16, R), F32),
             pltpu.VMEM((3, 16, R), F32),
-            pltpu.VMEM((8, 6, 16, R), F32),
+            pltpu.VMEM((8, 16, R), F32),
+            pltpu.VMEM((8, 5, 16, R), F32),
             pltpu.VMEM((7,) + block, BF16),
             pltpu.VMEM((8,) + block, BF16),
             pltpu.VMEM((2 * R, R), F32),
@@ -620,12 +661,13 @@
             pltpu.VMEM((8, 16, R), F32),
             dma((3,)), dma((3,)),
             dma((2, 8)), dma((2, 3)),
-            dma((8,)), dma,
+            dma((2, 8)), dma((2,)),
             dma((8,)), dma((8,)),
             dma((8,)), dma((8,)),
             dma((8,)), dma((8,)),
             dma((4,)), dma((4,)),
             dma((8,)), dma,
+            dma((8,)), dma((8,)),
             dma((8,)), dma((8,)),
             dma((8,)), dma((8,)),
             dma((8,)), dma((8,)),

time: 55.5 us -> 55.9 us (level)
  no operation moved by 1% of the time
where the time goes in v5:
time: 55.9 us; the launch traced here: 55.6 us
  Pallas kernels  55.6 us (99%)
    pallas_call x1, Pallas kernels, tree(): pl.pallas_call(tree_kernel, out_shape=jax.ShapeDtypeStruct((LEAVES, LEAF,...  50.7 us
    pallas_call x1, Pallas kernels, scatter(): pl.pallas_call(scatter_kernel, out_shape=jax.ShapeDtypeStruct((PTS, R), B...  4.87 us

profile of v5, /device:TPU:1, one launch (start us, length us, event | category | flops | bytes accessed | tf_op | source)
XLA Modules:
  0.0 55.6 jit_solution(7411674017327162274)
XLA Ops:
  0.0 50.7 %tree.1.total = bf16[16,256,128]{2,1,0:T(8,128)(2,1)} custom-call(s32[1,3072]{1,0:T(1,128)} %order.3, s32[1,16]{1,0:T(1,128)} %sizes.3, bf16[3072,128]{1,0:T(8,128)(2,1)} %v_ref.1, f32[8,3072]{1,0:T(8,128)} %p_ref.1, bf16[16,256,128]{2,1,0:T(8,128)(2,1)} %basis_any.1, bf16[15,256,128]{2,1,0:T(8,128)(2,1)} %bitcast.1, bf16[15,128,128]{2,1,0:T(8,128)(2,1)} %coupling_any.1, ...), custom_call_target="tpu_custom_call" | custom-call | tf_op jit(solution)/shard_map/tree/pallas_call | solution.py:616
  50.7 4.9 %scatter_rows.1 = bf16[3072,128]{1,0:T(8,128)(2,1)} custom-call(s32[1,3072]{1,0:T(1,128)} %order.3, s32[1,16]{1,0:T(1,128)} %sizes.3, bf16[16,256,128]{2,1,0:T(8,128)(2,1)} %tree.1.total), custom_call_target="tpu_custom_call" | custom-call | tf_op jit(solution)/shard_map/scatter_rows/pallas_call | solution.py:64

commit v6 on v5

--- a/solution.py
+++ b/solution.py
@@ -128,8 +128,8 @@
 
 
 def tree_kernel(
-    order, sizes, v_ref, p_ref, basis_any, transfer_any, coupling_any, ctrans, ccoup, total,
-    v_in, p_in, basis, transfer, coupling, s_local, tv, tp, gv, gp, rows, pts,
+    order, sizes, v_ref, p_ref, basis_any, transfer_any, coupling_any, ctrans, ccoup, total_any,
+    total, s_total, v_in, p_in, basis, transfer, coupling, s_local, tv, tp, gv, gp, rows, pts,
     coef, term, field, near, own, core_mats, core_coef, up_field,
     path, piece, wpiece, wlev, xpiece, xpath, w8lev, xlev, mat_w, mat_c,
     far, prod, yslice, yblock, zsend, zgot, xsend, xgot, gdown, fdown,
@@ -294,7 +294,7 @@
                 m1(k, 1).start()
             piece[z] = own[:, 0:16, :]
 
-        for level in (2,):
+        for level in range(3):
             size = 2 << level
 
             @pl.when(lax.rem(y, size) == size // 2)
@@ -323,19 +323,6 @@
         lax.fori_loop(first // UNROLL, last // UNROLL, move, 0)
 
     permute(tv, gv, 0, PTS)
-
-    @pl.when(is0)
-    def _():
-        for level in (1, 0):
-            size = 2 << level
-
-            @pl.when(lax.rem(y, size) == size // 2)
-            def _():
-                for c in direct_all(level, 0):
-                    c.start()
-                path[level, 0] = own[1]
-                path[level, 1] = own[2]
-
 
     slot = lax.broadcasted_iota(jnp.int32, (LEAF, R), 0)
     starts = [0]
@@ -491,7 +478,7 @@
         for m in FAR_FIRST:
             yb(m).start()
 
-    lax.fori_loop(4, 12, nearby, 0, unroll=8)
+    lax.fori_loop(4, LEAVES, nearby, 0, unroll=4)
 
     @pl.when(is0)
     def _():
@@ -508,11 +495,6 @@
         xsend[1] = mm(u, mat_w[6])
         for m in (2, 3, 1):
             xs(m).start()
-
-    lax.fori_loop(12, LEAVES, nearby, 0, unroll=4)
-
-    @pl.when(is0)
-    def _():
         for m in range(1, 8):
             m5_from(m).wait_recv()
         sides = [lax.rem(lax.div(z, 1 << i), 2) for i in range(3)] + [lax.rem(x, 2), lax.div(x, 2)]
@@ -571,8 +553,16 @@
         field[2 * j] = both[:, :R] + term[2 * j]
         field[2 * j + 1] = both[:, R:] + term[2 * j + 1]
 
+    saves = []
     for t in range(LEAVES):
         total[t] = (near[t] + dot(basis[t], field[t].astype(BF16), 1, 1)).astype(BF16)
+        if t % 4 == 3:
+            saves.append(
+                pltpu.make_async_copy(total.at[t - 3 : t + 1], total_any.at[t - 3 : t + 1], s_total.at[t // 4])
+            )
+            saves[-1].start()
+    for save in saves:
+        save.wait()
 
     @pl.when(is1)
     def _():
@@ -617,8 +607,10 @@
         tree_kernel,
         out_shape=jax.ShapeDtypeStruct((LEAVES, LEAF, R), BF16),
         in_specs=[SMEM, SMEM, HBM, HBM, HBM, HBM, HBM, VMEM, VMEM],
-        out_specs=VMEM,
+        out_specs=HBM,
         scratch_shapes=[
+            pltpu.VMEM((LEAVES, LEAF, R), BF16),
+            dma((4,)),
             pltpu.VMEM((PTS, R), BF16),
             pltpu.VMEM((8, PTS), F32),
             pltpu.VMEM((LEAVES, LEAF, R), BF16),

time: 55.9 us -> 55.4 us (level)
  no operation moved by 1% of the time
where the time goes in v6:
time: 55.4 us; the launch traced here: 55.1 us
  Pallas kernels  55.1 us (99%)
    pallas_call x1, Pallas kernels, tree(): pl.pallas_call(tree_kernel, out_shape=jax.ShapeDtypeStruct((LEAVES, LEAF,...  50.2 us
    pallas_call x1, Pallas kernels, scatter(): pl.pallas_call(scatter_kernel, out_shape=jax.ShapeDtypeStruct((PTS, R), B...  4.87 us

profile of v6, /device:TPU:1, one launch (start us, length us, event | category | flops | bytes accessed | tf_op | source)
XLA Modules:
  0.0 55.1 jit_solution(3261526779504057718)
XLA Ops:
  0.0 50.2 %tree.1.total = bf16[16,256,128]{2,1,0:T(8,128)(2,1)} custom-call(s32[1,3072]{1,0:T(1,128)} %order.3, s32[1,16]{1,0:T(1,128)} %sizes.3, bf16[3072,128]{1,0:T(8,128)(2,1)} %v_ref.1, f32[8,3072]{1,0:T(8,128)} %p_ref.1, bf16[16,256,128]{2,1,0:T(8,128)(2,1)} %basis_any.1, bf16[15,256,128]{2,1,0:T(8,128)(2,1)} %bitcast.1, bf16[15,128,128]{2,1,0:T(8,128)(2,1)} %coupling_any.1, ...), custom_call_target="tpu_custom_call" | custom-call | tf_op jit(solution)/shard_map/tree/pallas_call | solution.py:606
  50.3 4.9 %scatter_rows.1 = bf16[3072,128]{1,0:T(8,128)(2,1)} custom-call(s32[1,3072]{1,0:T(1,128)} %order.3, s32[1,16]{1,0:T(1,128)} %sizes.3, bf16[16,256,128]{2,1,0:T(8,128)(2,1)} %tree.1.total), custom_call_target="tpu_custom_call" | custom-call | tf_op jit(solution)/shard_map/scatter_rows/pallas_call | solution.py:64
